TPU v7x, 256 devices: a whole 4x4x8 slice. The times are simulated.
256 devices in a mesh: tm: 64 (over y_lo, x, z), rows: 4 (over y_hi, core).
Axes of the slice: x: 4, y: 4 (y_hi: 2, y_lo: 2; y = y_hi * 2 + y_lo), z: 8, core: 2. Of those that a mesh axis runs over, the one named last changes fastest.
Arguments:
- latents: bfloat16 [128, 24, 24, 1280], P('tm', 'rows'), may hold values from -40 to 40
- reference_features: bfloat16 [4608, 1280], P(('tm', 'rows')), may hold values from -12 to 12
- norm_gain: float32 [1280], replicated, may hold values from 0.2 to 5
- query_weight: bfloat16 [1280, 640], replicated, may hold values from -3 to 3
- key_weight: bfloat16 [1280, 640], replicated, may hold values from -3 to 3
- value_weight: bfloat16 [1280, 640], replicated, may hold values from -0.15625 to 0.15625
- out_weight: bfloat16 [640, 1280], replicated, may hold values from -1 to 1
- out_bias: float32 [1280], replicated, may hold values from -3 to 3
- motion_gain: float32 [1280], replicated, may hold values from 0.1 to 1.9
- motion_query: bfloat16 [1280, 640], replicated, may hold values from -3 to 3
- motion_key: bfloat16 [1280, 640], replicated, may hold values from -3 to 3
- motion_value: bfloat16 [1280, 640], replicated, may hold values from -0.15625 to 0.15625
Outputs:
- block_out: bfloat16 [128, 24, 24, 1280], P('tm', 'rows')
- motion_heads: bfloat16 [128, 24, 24, 640], P('tm', 'rows')
All inputs are finite; a program needn't handle non-finite values.
Results may differ from a plain program's by a relative error of at most 0.018.
Values may be sent and summed in bfloat16 or wider, within the bound.
No kernel may reach another device: no remote copies, remote signals or barrier semaphores. Data moves between devices by JAX's collectives and lax.ppermute only.
A program may use at most 128 MiB of HBM per device.

v0:
```python
import math

import jax
import jax.numpy as jnp
from jax import lax
from jax.sharding import PartitionSpec as P

GROUPS = 32
HEADS = 4
HD = 160
THEADS = 4
THD = 160
SHOT_BITS = 3


def swapped(value, axis, distance):
    mask = 2**distance
    pairs = [(source, source ^ mask) for source in range(lax.axis_size(axis))]
    return lax.ppermute(value, axis, pairs)


def position_codes(positions, channels):
    halves = jnp.arange(channels // 2, dtype=jnp.float32)
    rates = jnp.exp(-math.log(10000.0) * 2.0 * halves / channels)
    angles = positions[:, None] * rates[None, :]
    return jnp.stack([jnp.sin(angles), jnp.cos(angles)], axis=-1).reshape(
        positions.shape[0], channels
    )


def frame_attention(motion_q, motion_k, motion_v):
    query_count, cells = (motion_q.shape[0], motion_q.shape[1])
    query_heads = motion_q.reshape(query_count, cells, THEADS, THD)
    key_heads = motion_k.reshape(motion_k.shape[0], cells, THEADS, THD)
    value_heads = motion_v.reshape(motion_v.shape[0], cells, THEADS, THD)
    scores = jnp.einsum(
        "fphd,gphd->phfg", query_heads, key_heads, preferred_element_type=jnp.float32
    ) / math.sqrt(THD)
    highest = jnp.max(scores, axis=-1, keepdims=True)
    exps = jnp.exp(scores - highest)
    totals = jnp.sum(exps, axis=-1)
    mixed = jnp.einsum(
        "phfg,gphd->fphd",
        exps.astype(jnp.bfloat16),
        value_heads,
        preferred_element_type=jnp.float32,
    )
    mixed = mixed / jnp.transpose(totals, (2, 0, 1))[..., None]
    return mixed.astype(jnp.bfloat16).reshape(query_count, cells, THEADS * THD)


def body(
    latents,
    reference_features,
    norm_gain,
    query_weight,
    key_weight,
    value_weight,
    out_weight,
    out_bias,
    motion_gain,
    motion_query,
    motion_key,
    motion_value,
):
    frames, row_count, col_count, channels = latents.shape
    places = row_count * col_count
    head_width = HEADS * HD
    motion_width = THEADS * THD
    device_index = lax.axis_index("tm")
    bit_order = list(range(SHOT_BITS))
    grouped = latents.astype(jnp.float32).reshape(frames, places, GROUPS, channels // GROUPS)
    group_sums = jnp.sum(grouped, axis=(1, 3))
    group_squares = jnp.sum(grouped * grouped, axis=(1, 3))
    group_sums, group_squares = lax.psum((group_sums, group_squares), "rows")
    group_cells = places * lax.axis_size("rows") * (channels // GROUPS)
    group_mean = group_sums / group_cells
    group_var = group_squares / group_cells - group_mean * group_mean
    normed = (grouped - group_mean[:, None, :, None]) * lax.rsqrt(group_var + 1e-05)[
        :, None, :, None
    ]
    normed = (normed.reshape(frames, places, channels) * norm_gain).astype(jnp.bfloat16)
    flat_normed = normed.reshape(frames * places, channels)
    queries = jnp.dot(flat_normed, query_weight, preferred_element_type=jnp.float32).astype(
        jnp.bfloat16
    )
    queries = queries.reshape(frames, places, HEADS, HD)
    frame_keys = jnp.dot(flat_normed, key_weight, preferred_element_type=jnp.float32).astype(
        jnp.bfloat16
    )
    frame_values = jnp.dot(flat_normed, value_weight, preferred_element_type=jnp.float32).astype(
        jnp.bfloat16
    )
    frame_keys = frame_keys.reshape(frames, places, head_width)
    frame_values = frame_values.reshape(frames, places, head_width)
    ref_key_part = jnp.dot(
        reference_features, key_weight, preferred_element_type=jnp.float32
    ).astype(jnp.bfloat16)
    ref_value_part = jnp.dot(
        reference_features, value_weight, preferred_element_type=jnp.float32
    ).astype(jnp.bfloat16)
    ref_pair = jnp.stack([ref_key_part, ref_value_part])
    for bit_number in bit_order:
        ref_pair = jnp.concatenate([ref_pair, swapped(ref_pair, "tm", bit_number)], axis=1)
    ref_pair = lax.all_gather(ref_pair, "rows", axis=1, tiled=True)
    ref_keys = ref_pair[0].reshape(-1, HEADS, HD)
    ref_values = ref_pair[1].reshape(-1, HEADS, HD)
    score_scale = 1.0 / math.sqrt(HD)
    whole_places = places * lax.axis_size("rows")
    ref_scores = (
        jnp.einsum("fphd,khd->fhpk", queries, ref_keys, preferred_element_type=jnp.float32)
        * score_scale
    )
    key_piece = lax.all_gather(frame_keys, "rows", axis=1, tiled=True).reshape(
        frames, -1, HEADS, HD
    )
    scores = (
        jnp.einsum("fphd,fkhd->fhpk", queries, key_piece, preferred_element_type=jnp.float32)
        * score_scale
    )
    value_buffer = lax.all_gather(frame_values, "rows", axis=1, tiled=True)
    top = jnp.maximum(jnp.max(ref_scores, axis=-1), jnp.max(scores, axis=-1))
    ref_exps = jnp.exp(ref_scores - top[..., None])
    frame_exps = jnp.exp(scores - top[..., None])
    total = jnp.sum(ref_exps, axis=-1) + jnp.sum(frame_exps, axis=-1)
    frame_value_heads = value_buffer.reshape(frames, whole_places, HEADS, HD)
    summed = jnp.einsum(
        "fhpk,khd->fhpd",
        ref_exps.astype(jnp.bfloat16),
        ref_values,
        preferred_element_type=jnp.float32,
    )
    summed = summed + jnp.einsum(
        "fhpk,fkhd->fhpd",
        frame_exps.astype(jnp.bfloat16),
        frame_value_heads,
        preferred_element_type=jnp.float32,
    )
    attended = summed / total[..., None]
    attended = (
        jnp.transpose(attended, (0, 2, 1, 3))
        .astype(jnp.bfloat16)
        .reshape(frames * places, head_width)
    )
    block = (
        latents.astype(jnp.float32).reshape(frames * places, channels)
        + jnp.dot(attended, out_weight, preferred_element_type=jnp.float32)
        + out_bias
    )
    block_out = block.astype(jnp.bfloat16)
    block_wide = block_out.astype(jnp.float32).reshape(frames, places, channels)
    cell_mean = jnp.mean(block_wide, axis=-1, keepdims=True)
    centered = block_wide - cell_mean
    cell_var = jnp.mean(centered * centered, axis=-1, keepdims=True)
    shot_frames = frames * 2**SHOT_BITS
    frame_ids = device_index * frames + jnp.arange(frames, dtype=jnp.int32)
    frame_pos = (frame_ids % shot_frames).astype(jnp.float32)
    codes = position_codes(frame_pos, channels)
    motion_in = (centered * lax.rsqrt(cell_var + 1e-05) * motion_gain + codes[:, None, :]).astype(
        jnp.bfloat16
    )
    motion_flat = motion_in.reshape(frames * places, channels)
    motion_q = jnp.dot(motion_flat, motion_query, preferred_element_type=jnp.float32).astype(
        jnp.bfloat16
    )
    motion_k = jnp.dot(motion_flat, motion_key, preferred_element_type=jnp.float32).astype(
        jnp.bfloat16
    )
    motion_v = jnp.dot(motion_flat, motion_value, preferred_element_type=jnp.float32).astype(
        jnp.bfloat16
    )
    motion_q = motion_q.reshape(frames, places, motion_width)
    motion_k = motion_k.reshape(frames, places, motion_width)
    motion_v = motion_v.reshape(frames, places, motion_width)
    motion_pair = jnp.stack([motion_k, motion_v])
    for bit_number in bit_order:
        motion_pair = jnp.concatenate([motion_pair, swapped(motion_pair, "tm", bit_number)], axis=1)
    motion_heads = frame_attention(motion_q, motion_pair[0], motion_pair[1])
    return (
        block_out.reshape(frames, row_count, col_count, channels),
        motion_heads.reshape(frames, row_count, col_count, motion_width),
    )


def solution(mesh):
    return jax.shard_map(
        body,
        mesh=mesh,
        in_specs=(
            P("tm", "rows", None, None),
            P(("tm", "rows"), None),
            P(),
            P(),
            P(),
            P(),
            P(),
            P(),
            P(),
            P(),
            P(),
            P(),
        ),
        out_specs=(P("tm", "rows", None, None), P("tm", "rows", None, None)),
        check_vma=False,
    )
```

profile of v0, /device:TPU:2, one launch (start us, length us, event | category | flops | bytes accessed | tf_op | source)
XLA Modules:
  0.0 387.2 jit_solution(1599538494100854348)
XLA Ops:
  7.2 1.5 convert_reduce_fusion.1
  9.1 10.1 %all-reduce = (f32[2,32]{1,0:T(2,128)S(1)}, f32[2,32]{1,0:T(2,128)S(1)}) all-reduce(f32[2,32]{1,0:T(2,128)S(1)} %reduce_sum.82, f32[2,32]{1,0:T(2,128)S(1)} %reduce_sum.79), channel_id=1, replica_groups=mesh['tm'=64,'rows'=4] {'rows'}, use_global_device_ids=true, to_apply=%region_5.0 | all-reduce | flops 128 | bytes 1024 | tf_op jit(solution)/shard_map/psum | solution.py:75
  19.6 1.3 fusion.25
  21.8 1.0 copy.116
  22.9 3.2 convolution_convert_fusion.4
  26.5 1.1 copy-done.7
  27.9 2.0 collective-permute-start
  29.9 2.3 collective-permute-done
  32.3 3.8 collective-permute-start.1
  36.1 3.7 collective-permute-done.1
  39.9 11.1 %collective-permute-start.2 = (bf16[2,72,640]{2,1,0:T(8,128)(2,1)S(1)}, bf16[2,72,640]{2,1,0:T(8,128)(2,1)S(1)}, u32[]{:S(2)}, u32[]{:S(2)}) collective-permute-start(bf16[2,72,640]{2,1,0:T(8,128)(2,1)S(1)} %pad_maximum_fusion.5), channel_id=1, source_target_pairs={{0,16},{4,20},{8,24},{12,28},{16,0},{20,4},{24,8},{28,12},{32,48},... | collective-permute-start | bytes 552968 | tf_op jit(solution)/shard_map/ppermute | solution.py:19
  51.0 3.5 collective-permute-done.2
  54.5 0.8 pad_maximum_fusion.4
  56.3 2.2 convolution_convert_fusion.5
  58.9 1.0 copy.112
  59.9 3.6 copy.117
  63.5 12.9 %all-gather.6.cloned.1.call-done = bf16[2,576,640]{2,1,0:T(8,128)(2,1)} async-done(((bf16[2,144,640]{2,1,0:T(8,128)(2,1)}), bf16[2,576,640]{2,1,0:T(8,128)(2,1)}) %all-gather.6.cloned.1.call-update) | async-done | bytes 1474576 | tf_op jit(solution)/shard_map/all_gather | solution.py:114
  76.5 2.6 copy.113
  79.1 3.8 multiply_reduce_fusion
  83.0 20.5 %all-gather.4.cloned.1.call-done = bf16[2,576,640]{2,1,0:T(8,128)(2,1)} async-done(((bf16[2,144,640]{2,1,0:T(8,128)(2,1)}), bf16[2,576,640]{2,1,0:T(8,128)(2,1)}) %all-gather.4.cloned.1.call-update) | async-done | bytes 1474576 | tf_op jit(solution)/shard_map/all_gather | solution.py:105
  103.5 2.6 fusion.60
  106.1 2.3 copy.110
  108.4 2.3 copy.111
  110.7 1.9 fusion.62
  113.0 1.4 copy-done.2
  114.5 1.2 fusion.7
  115.7 0.8 fusion.36
  116.9 0.9 divide_convert_fusion
  118.8 0.9 convert_reduce_fusion
  120.5 0.9 copy-done.16
  123.7 1.6 collective-permute-start.3
  125.4 17.1 %collective-permute-done.3 = bf16[2,2,144,640]{3,2,1,0:T(8,128)(2,1)S(1)} collective-permute-done((bf16[2,2,144,640]{3,2,1,0:T(8,128)(2,1)S(1)}, bf16[2,2,144,640]{3,2,1,0:T(8,128)(2,1)S(1)}, u32[]{:S(2)}, u32[]{:S(2)}) %collective-permute-start.3) | collective-permute-done | bytes 737312 | tf_op jit(solution)/shard_map/ppermute | solution.py:19
  142.6 2.8 collective-permute-start.4
  145.5 63.6 %collective-permute-done.4 = bf16[2,4,144,640]{3,2,1,0:T(8,128)(2,1)S(1)} collective-permute-done((bf16[2,4,144,640]{3,2,1,0:T(8,128)(2,1)S(1)}, bf16[2,4,144,640]{3,2,1,0:T(8,128)(2,1)S(1)}, u32[]{:S(2)}, u32[]{:S(2)}) %collective-permute-start.4) | collective-permute-done | bytes 1474592 | tf_op jit(solution)/shard_map/ppermute | solution.py:19
  209.0 1.8 pad_maximum_fusion.1
  210.8 5.7 %collective-permute-start.5 = (bf16[2,8,144,640]{3,2,1,0:T(8,128)(2,1)}, bf16[2,8,144,640]{3,2,1,0:T(8,128)(2,1)}, u32[]{:S(2)}, u32[]{:S(2)}) collective-permute-start(bf16[2,8,144,640]{3,2,1,0:T(8,128)(2,1)} %pad_maximum_fusion.1), channel_id=1, source_target_pairs={{0,16},{4,20},{8,24},{12,28},{16,0},{20,4},{24,8},{28,12},{32,48},... | collective-permute-start | bytes 8847368 | tf_op jit(solution)/shard_map/ppermute | solution.py:19
  216.6 1.5 convolution_convert_fusion
  218.1 1.4 reshape_reshape.6
  219.5 125.3 %collective-permute-done.5 = bf16[2,8,144,640]{3,2,1,0:T(8,128)(2,1)} collective-permute-done((bf16[2,8,144,640]{3,2,1,0:T(8,128)(2,1)}, bf16[2,8,144,640]{3,2,1,0:T(8,128)(2,1)}, u32[]{:S(2)}, u32[]{:S(2)}) %collective-permute-start.5) | collective-permute-done | bytes 2949152 | tf_op jit(solution)/shard_map/ppermute | solution.py:19
  344.8 2.9 pad_maximum_fusion
  347.7 2.1 fusion.59
  349.9 10.1 %reshape_squeeze.15 = bf16[16,144,4,160]{3,2,1,0:T(4,128)(2,1)} reshape(bf16[1,16,144,640]{3,2,1,0:T(8,128)(2,1)} %get-tuple-element.8) | data formatting | bytes 5898240 | tf_op jit(solution)/shard_map/reshape;squeeze | solution.py:34
  360.0 5.8 %fusion.61 = (f32[144,4,2]{2,1,0:T(4,128)S(1)}, f32[144,4,2,16]{3,2,1,0:T(2,128)S(1)}) fusion(bf16[16,144,4,160]{3,2,1,0:T(4,128)(2,1)} %reshape_squeeze.15, bf16[2,144,4,160]{3,2,1,0:T(4,128)(2,1)S(1)} %reshape_reshape.6), kind=kOutput, calls=%fused_computation.88 | convolution fusion | flops 5933952 | bytes 3396096 | tf_op jit(solution)/shard_map/fphd,gphd->phfg/dot_general | solution.py:36
  365.8 0.8 copy-done.11
  366.6 1.5 fusion.50
  368.3 4.8 %reshape_squeeze.14 = bf16[16,144,4,160]{3,2,1,0:T(4,128)(2,1)} reshape(bf16[1,16,144,640]{3,2,1,0:T(8,128)(2,1)S(1)} %get-tuple-element.9) | data formatting | bytes 5898240 | tf_op jit(solution)/shard_map/reshape;squeeze | solution.py:35
  373.1 5.8 %fusion = f32[144,4,160,2]{2,3,1,0:T(2,128)S(1)} fusion(bf16[16,144,4,160]{3,2,1,0:T(4,128)(2,1)} %reshape_squeeze.14, f32[144,4,2,16]{3,2,1,0:T(2,128)S(1)} %copy-done.12, f32[144,4,2]{2,1,0:T(4,128)} %copy-done.13), kind=kOutput, calls=%fused_computation.1 | convolution fusion | flops 5935104 | bytes 3764736 | tf_op jit(solution)/shard_map/phfg,gphd->fphd/dot_general | solution.py:42
  379.6 1.1 reshape_reshape.7
  (81 shorter events, 9.7 us)
Async XLA Ops:
  7.2 111.4 %copy-start = (bf16[640,1280]{1,0:T(8,128)(2,1)S(1)}, bf16[640,1280]{1,0:T(8,128)(2,1)}, u32[]{:S(2)}) copy-start(bf16[640,1280]{1,0:T(8,128)(2,1)} %param.18) | copy-start | bytes 4915204
  7.2 13.7 %copy-start.6 = (bf16[1280,640]{1,0:T(8,128)(2,1)S(1)}, bf16[1280,640]{1,0:T(8,128)(2,1)}, u32[]{:S(2)}) copy-start(bf16[1280,640]{1,0:T(8,128)(2,1)} %param.17) | copy-start | bytes 4915204
  7.2 52.7 %all-gather.8.cloned.1.call-start = ((), (), s32[]{:S(2)}) async-start(), calls=%async_computation.2 | async-start | bytes 1843200 | tf_op jit(solution)/shard_map/all_gather | solution.py:121
  20.9 0.9 copy-start.9
  22.8 3.3 copy-start.14
  22.8 53.7 %all-gather.6.cloned.1.call-start = ((), (), s32[]{:S(2)}) async-start(), calls=%async_computation.1 | async-start | bytes 1843200 | tf_op jit(solution)/shard_map/all_gather | solution.py:114
  26.1 77.4 %all-gather.4.cloned.1.call-start = ((), (), s32[]{:S(2)}) async-start(), calls=%async_computation | async-start | bytes 1843200 | tf_op jit(solution)/shard_map/all_gather | solution.py:105
  26.1 1.4 copy-start.7
  27.9 28.4 %copy-start.10 = (bf16[288,1280]{1,0:T(8,128)(2,1)S(1)}, bf16[288,1280]{1,0:T(8,128)(2,1)}, u32[]{:S(2)}) copy-start(bf16[288,1280]{1,0:T(8,128)(2,1)} %copy-done.9) | copy-start | bytes 2211844
  27.9 4.3 %collective-permute-start = (bf16[2,18,640]{2,1,0:T(8,128)(2,1)S(1)}, bf16[2,18,640]{2,1,0:T(8,128)(2,1)S(1)}, u32[]{:S(2)}, u32[]{:S(2)}) collective-permute-start(bf16[2,18,640]{2,1,0:T(8,128)(2,1)S(1)} %pad_maximum_fusion.7), channel_id=1, source_target_pairs={{0,4},{4,0},{8,12},{12,8},{16,20},{20,16},{24,28},{28,24},{32,36},... | collective-permute-start | bytes 138248 | tf_op jit(solution)/shard_map/ppermute | solution.py:19
  32.3 7.6 %collective-permute-start.1 = (bf16[2,36,640]{2,1,0:T(8,128)(2,1)S(1)}, bf16[2,36,640]{2,1,0:T(8,128)(2,1)S(1)}, u32[]{:S(2)}, u32[]{:S(2)}) collective-permute-start(bf16[2,36,640]{2,1,0:T(8,128)(2,1)S(1)} %pad_maximum_fusion.6), channel_id=1, source_target_pairs={{0,8},{4,12},{8,0},{12,4},{16,24},{20,28},{24,16},{28,20},{32,40},... | collective-permute-start | bytes 276488 | tf_op jit(solution)/shard_map/ppermute | solution.py:19
  39.9 14.6 %collective-permute-start.2 = (bf16[2,72,640]{2,1,0:T(8,128)(2,1)S(1)}, bf16[2,72,640]{2,1,0:T(8,128)(2,1)S(1)}, u32[]{:S(2)}, u32[]{:S(2)}) collective-permute-start(bf16[2,72,640]{2,1,0:T(8,128)(2,1)S(1)} %pad_maximum_fusion.5), channel_id=1, source_target_pairs={{0,16},{4,20},{8,24},{12,28},{16,0},{20,4},{24,8},{28,12},{32,48},... | collective-permute-start | bytes 552968 | tf_op jit(solution)/shard_map/ppermute | solution.py:19
  58.9 1.0 copy-start.3
  112.6 1.8 copy-start.2
  115.7 1.1 copy-start.8
  117.7 1.1 copy-start.4
  117.7 1.1 copy-start.19
  118.8 1.3 copy-start.15
  119.7 2.5 copy-start.5
  119.7 1.7 copy-start.16
  121.4 1.4 copy-start.17
  123.7 18.7 %collective-permute-start.3 = (bf16[2,2,144,640]{3,2,1,0:T(8,128)(2,1)S(1)}, bf16[2,2,144,640]{3,2,1,0:T(8,128)(2,1)S(1)}, u32[]{:S(2)}, u32[]{:S(2)}) collective-permute-start(bf16[2,2,144,640]{3,2,1,0:T(8,128)(2,1)S(1)} %pad_maximum_fusion.3), channel_id=1, source_target_pairs={{0,4},{4,0},{8,12},{12,8},{16,20},{20,16},{24,28},{28,24},{32,36},... | collective-permute-start | bytes 2211848 | tf_op jit(solution)/shard_map/ppermute | solution.py:19
  142.6 74.0 %copy-start.18 = (bf16[1280,640]{1,0:T(8,128)(2,1)S(1)}, bf16[1280,640]{1,0:T(8,128)(2,1)}, u32[]{:S(2)}) copy-start(bf16[1280,640]{1,0:T(8,128)(2,1)} %param.21) | copy-start | bytes 4915204
  142.6 66.4 %collective-permute-start.4 = (bf16[2,4,144,640]{3,2,1,0:T(8,128)(2,1)S(1)}, bf16[2,4,144,640]{3,2,1,0:T(8,128)(2,1)S(1)}, u32[]{:S(2)}, u32[]{:S(2)}) collective-permute-start(bf16[2,4,144,640]{3,2,1,0:T(8,128)(2,1)S(1)} %pad_maximum_fusion.2), channel_id=1, source_target_pairs={{0,8},{4,12},{8,0},{12,4},{16,24},{20,28},{24,16},{28,20},{32,40},... | collective-permute-start | bytes 4423688 | tf_op jit(solution)/shard_map/ppermute | solution.py:19
  210.8 134.0 %collective-permute-start.5 = (bf16[2,8,144,640]{3,2,1,0:T(8,128)(2,1)}, bf16[2,8,144,640]{3,2,1,0:T(8,128)(2,1)}, u32[]{:S(2)}, u32[]{:S(2)}) collective-permute-start(bf16[2,8,144,640]{3,2,1,0:T(8,128)(2,1)} %pad_maximum_fusion.1), channel_id=1, source_target_pairs={{0,16},{4,20},{8,24},{12,28},{16,0},{20,4},{24,8},{28,12},{32,48},... | collective-permute-start | bytes 8847368 | tf_op jit(solution)/shard_map/ppermute | solution.py:19
  365.8 0.8 copy-start.11
  365.8 2.3 copy-start.13
  368.3 4.8 %copy-start.12 = (f32[144,4,2,16]{3,2,1,0:T(2,128)S(1)}, f32[144,4,2,16]{3,2,1,0:T(2,128)}, u32[]{:S(2)}) copy-start(f32[144,4,2,16]{3,2,1,0:T(2,128)} %copy-done.11) | copy-start | bytes 221188
  373.1 7.6 %copy-start.1 = (bf16[640,1280]{1,0:T(8,128)(2,1)S(1)}, bf16[640,1280]{1,0:T(8,128)(2,1)}, u32[]{:S(2)}) copy-start(bf16[640,1280]{1,0:T(8,128)(2,1)} %param.18) | copy-start | bytes 4915204
Sparse Core Ops, SparseCore 0:
  22.9 26.5 all-gather.7
  51.3 25.1 all-gather.5
  78.3 25.1 all-gather.3
where the time goes:
time: 388 us; the launch traced here: 387 us
  waiting for transfers between devices  249 us (64%)
  local copies, waits for them, and re-layouts  43.7 us (11%)
  matrix products  29.6 us (8%)
  starting transfers between devices  27.3 us (7%)
  between operations  14.2 us (4%)
  other arithmetic  13.4 us (3%)
  blocking collectives  10.1 us (3%)
    ppermute x6, waiting for transfers between devices, swapped(): return lax.ppermute(value, axis, pairs)  216 us
    ppermute x6, starting transfers between devices, swapped(): return lax.ppermute(value, axis, pairs)  27.2 us
    all_gather x1, waiting for transfers between devices, body(): ref_pair = lax.all_gather(ref_pair, 'rows', axis=1, tiled=True)  20.5 us
    all_gather x1, waiting for transfers between devices, body(): lax.all_gather(frame_keys, 'rows', axis=1, tiled=True)  12.9 us
    another operation x1, local copies, waits for them, and re-layouts, frame_attention(): key_heads = motion_k.reshape(motion_k.shape[0], cells, THEADS, THD)  10.1 us
    psum x1, blocking collectives, body(): group_sums, group_squares = lax.psum((group_sums, group_squares), 'rows')  10.1 us
  transfers between devices with their start and end apart: 9, of which 8 were waited for; matrix products, arithmetic and copies ran while one was open for 6% of the time, Pallas kernels for 0%

commit v1 on v0

v1 whole, which is shorter than its diff:
```python
import functools
import math

import jax
import jax.numpy as jnp
import numpy as np
from jax import lax
from jax.experimental import pallas as pl
from jax.experimental.pallas import tpu as pltpu
from jax.sharding import PartitionSpec as P

GROUPS = 32
HEADS = 4
HD = 160
SHOT = 16
WINDOWS = tuple(HD * h // 128 * 128 for h in range(HEADS))
SCALE = math.log2(math.e) / math.sqrt(HD)
AXES = ("tm", "rows")
MAIN = 16
NT = (((1,), (1,)), ((), ()))
VMEM = 40 * 1024 * 1024


def mesh_perm(move):
    def flat(yl, x, z, yh, c):
        return ((yl * 4 + x) * 8 + z) * 4 + yh * 2 + c

    places = [
        (yl, x, z, yh, c)
        for yl in range(2)
        for x in range(4)
        for z in range(8)
        for yh in range(2)
        for c in range(2)
    ]
    return [(flat(*p), flat(*move(*p))) for p in places]


Y_FLIP = mesh_perm(lambda yl, x, z, yh, c: (yl, x, z, 1 - yh, c))
C_FLIP = mesh_perm(lambda yl, x, z, yh, c: (yl, x, z, yh, 1 - c))
YC_FLIP = mesh_perm(lambda yl, x, z, yh, c: (yl, x, z, 1 - yh, 1 - c))
Z_RING = mesh_perm(lambda yl, x, z, yh, c: (yl, x, (z + (1 if c == 0 else 7)) % 8, yh, c))


def send(value, pairs):
    return lax.ppermute(value, AXES, pairs)


def shot_groups():
    return [list(range(8 * g, 8 * g + 8)) for g in range(8)]


def exchange(value):
    return lax.all_to_all(value, "tm", 0, 0, axis_index_groups=shot_groups(), tiled=True)


def position_codes(channels):
    halves = np.arange(channels // 2, dtype=np.float64)
    rates = np.exp(-math.log(10000.0) * 2.0 * halves / channels)
    angles = np.arange(SHOT, dtype=np.float64)[:, None] * rates[None, :]
    return np.stack([np.sin(angles), np.cos(angles)], axis=-1).reshape(SHOT, channels).astype(
        np.float32
    )


def call(kernel, out_shape, args, in_specs=None, scratch=(), flops=0, moved=0):
    return pl.pallas_call(
        kernel,
        out_shape=out_shape,
        grid=(1,),
        in_specs=in_specs or [whole(a) for a in args],
        out_specs=jax.tree.map(whole, out_shape),
        scratch_shapes=scratch,
        compiler_params=pltpu.CompilerParams(vmem_limit_bytes=VMEM),
        cost_estimate=pl.CostEstimate(flops=flops, bytes_accessed=moved, transcendentals=0),
    )(*args)


def whole(a):
    rank = len(a.shape)
    return pl.BlockSpec(a.shape, lambda i: (0,) * rank)


def head_window(x, h):
    w = WINDOWS[h]
    part = x[:, w : w + 256]
    lane = lax.broadcasted_iota(jnp.int32, part.shape, 1)
    low = HD * h - w
    return jnp.where((lane >= low) & (lane < low + HD), part, jnp.zeros_like(part))


def side_by_side(parts):
    lane = lax.broadcasted_iota(jnp.int32, (parts[0].shape[0], 128), 1)
    cols = [parts[0][:, :128]]
    for h in range(1, HEADS):
        edge = HD * h - WINDOWS[h]
        cols.append(jnp.where(lane < edge, parts[h - 1][:, 128:], parts[h][:, :128]))
    cols.append(parts[HEADS - 1][:, 128:])
    return jnp.concatenate(cols, axis=1)


def dot(a, b):
    return jnp.dot(a, b, preferred_element_type=jnp.float32)


def group_stats(s1, s2, count):
    channels = s1.shape[1]
    width = channels // GROUPS
    ch = lax.broadcasted_iota(jnp.int32, (channels, 128), 0)
    gr = lax.broadcasted_iota(jnp.int32, (channels, 128), 1) * width
    member = jnp.where((ch >= gr) & (ch < gr + width), 1.0, 0.0)
    row = lax.broadcasted_iota(jnp.int32, (8, channels), 0)
    both = jnp.where(row == 0, s1, jnp.where(row == 1, s2, 0.0))
    sums = jnp.dot(both, member, precision=lax.Precision.HIGHEST) / count
    mean, square = sums[0:1], sums[1:2]
    rstd = lax.rsqrt(square - mean * mean + 1e-05)
    row = lax.broadcasted_iota(jnp.int32, (8, 128), 0)
    both = jnp.where(row == 0, mean, jnp.where(row == 1, rstd, 0.0))
    spread = lax.dot_general(both, member, NT, precision=lax.Precision.HIGHEST)
    return spread[0:1], spread[1:2]


def own_kernel(own, peer_c, peer_y, peer_yc, gain, wq, wk, wv, q_out, o_out, ml_out, xn, k, v):
    pieces = (own, peer_c, peer_y, peer_yc)
    places, channels = own.shape
    s1 = jnp.zeros((1, channels), jnp.float32)
    s2 = jnp.zeros((1, channels), jnp.float32)
    for piece in pieces:
        x = piece[...].astype(jnp.float32)
        s1 += jnp.sum(x, axis=0, keepdims=True)
        s2 += jnp.sum(x * x, axis=0, keepdims=True)
    mean, rstd = group_stats(s1, s2, 4 * places * (channels // GROUPS))
    for i, piece in enumerate(pieces):
        x = piece[...].astype(jnp.float32)
        xn[i * places : (i + 1) * places, :] = ((x - mean) * rstd * gain[...]).astype(jnp.bfloat16)
    q = dot(xn[:places, :], wq[...]).astype(jnp.bfloat16)
    q_out[...] = q
    k[...] = dot(xn[...], wk[...]).astype(jnp.bfloat16)
    v[...] = dot(xn[...], wv[...]).astype(jnp.bfloat16)
    lane = lax.broadcasted_iota(jnp.int32, (places, 128), 1)
    ml = jnp.zeros((places, 128), jnp.float32)
    for h in range(HEADS):
        w = WINDOWS[h]
        s = lax.dot_general(
            head_window(q, h), k[:, w : w + 256], NT, preferred_element_type=jnp.float32
        )
        top = jnp.max(s, axis=1, keepdims=True)
        p = jnp.exp2((s - top) * SCALE)
        total = jnp.sum(p, axis=1, keepdims=True)
        o_out[h] = dot(p.astype(jnp.bfloat16), v[:, w : w + 256])
        ml = jnp.where(lane == h, top, jnp.where(lane == HEADS + h, total, ml))
    ml_out[...] = ml


def ref_kernel(t0, t1, t2, t3, t4, t5, t6, t7, wk, wv, k_out, v_out):
    x = jnp.concatenate([t[...] for t in (t0, t1, t2, t3, t4, t5, t6, t7)], axis=0)
    k_out[...] = dot(x, wk[...]).astype(jnp.bfloat16)
    v_out[...] = dot(x, wv[...]).astype(jnp.bfloat16)


def join_kernel(q0, o0, ml0, q1, o1, ml1, rk, rv, att_out, packed, tail):
    places = q0.shape[0]
    for f, (q, o, ml) in enumerate(((q0, o0, ml0), (q1, o1, ml1))):
        parts = []
        for h in range(HEADS):
            w = WINDOWS[h]
            s = lax.dot_general(
                head_window(q[...], h), rk[:, w : w + 256], NT, preferred_element_type=jnp.float32
            )
            before = ml[:, h : h + 1]
            top = jnp.maximum(before, jnp.max(s, axis=1, keepdims=True))
            p = jnp.exp2((s - top) * SCALE)
            keep = jnp.exp2((before - top) * SCALE)
            total = ml[:, HEADS + h : HEADS + h + 1] * keep + jnp.sum(p, axis=1, keepdims=True)
            mixed = o[h] * keep + dot(p.astype(jnp.bfloat16), rv[:, w : w + 256])
            parts.append(mixed / total)
        att = side_by_side(parts)
        att_out[f] = att.astype(jnp.bfloat16)
        for d in range(8):
            packed[d, MAIN * f : MAIN * f + MAIN, :] = att_out[f, MAIN * d : MAIN * d + MAIN, :]
        tail[f] = att[8 * MAIN :, :]
    pack_tail(tail, packed, 2 * MAIN)


def pack_tail(tail, packed, base):
    width = tail.shape[2]
    for d in range(8):
        rows = [tail[f, 2 * d : 2 * d + 2, :] for f in range(2)]
        rows.append(jnp.zeros((4, width), jnp.float32))
        packed[d, base : base + 8, :] = jnp.concatenate(rows, axis=0).astype(jnp.bfloat16)


def pack_kernel(lat, packed, tail):
    half = lat.shape[2] // 2
    for f in range(2):
        for s in range(2):
            for d in range(8):
                at = 2 * MAIN * s + MAIN * f
                packed[d, at : at + MAIN, :] = lat[
                    f, MAIN * d : MAIN * d + MAIN, half * s : half * s + half
                ]
        tail[f] = lat[f, 8 * MAIN :, :].astype(jnp.float32)
    for d in range(8):
        rows = [
            tail[f, 2 * d : 2 * d + 2, half * s : half * s + half]
            for s in range(2)
            for f in range(2)
        ]
        packed[d, 4 * MAIN : 4 * MAIN + 8, :] = jnp.concatenate(rows, axis=0).astype(jnp.bfloat16)


def block_kernel(lat, att, wo, bias, out):
    for f in range(2):
        out[f] = (
            lat[f].astype(jnp.float32) + dot(att[f], wo[...]) + bias[...]
        ).astype(jnp.bfloat16)


def layer_norm(x, gain, codes):
    mean = jnp.mean(x, axis=-1, keepdims=True)
    centered = x - mean
    var = jnp.mean(centered * centered, axis=-1, keepdims=True)
    return centered * lax.rsqrt(var + 1e-05) * gain + codes


def masked_attention(q, k, v, same):
    parts = []
    for h in range(HEADS):
        w = WINDOWS[h]
        s = lax.dot_general(
            head_window(q, h), k[:, w : w + 256], NT, preferred_element_type=jnp.float32
        )
        s = jnp.where(same, s, -jnp.inf)
        top = jnp.max(s, axis=1, keepdims=True)
        p = jnp.exp2((s - top) * SCALE)
        total = jnp.sum(p, axis=1, keepdims=True)
        parts.append(dot(p.astype(jnp.bfloat16), v[:, w : w + 256]) / total)
    return side_by_side(parts)


def motion_kernel(
    lat, att, wo, bias, gain, codes, tail_codes, wq, wk, wv, out, x, q, k, v
):
    half = lat.shape[2]
    channels = 2 * half
    main_rows = 8 * 2 * MAIN
    tail_rows = 64
    main_att = att[:, : 2 * MAIN, :].reshape(main_rows, half)
    tail_att = att[:, 2 * MAIN :, :].reshape(tail_rows, half)
    main_left = lat[:, : 2 * MAIN, :].reshape(main_rows, half).astype(jnp.float32)
    main_right = lat[:, 2 * MAIN : 4 * MAIN, :].reshape(main_rows, half).astype(jnp.float32)
    tail_left = lat[:, 4 * MAIN :, :].reshape(tail_rows, half).astype(jnp.float32)
    tail_right = pltpu.roll(tail_left, tail_rows - 4, 0)
    main = jnp.concatenate([main_left, main_right], axis=1) + dot(main_att, wo[...]) + bias[...]
    main = main.astype(jnp.bfloat16).astype(jnp.float32)
    code_rows = jnp.broadcast_to(codes[...][:, None, :], (SHOT, MAIN, channels))
    x[:main_rows, :] = layer_norm(
        main, gain[...], code_rows.reshape(main_rows, channels)
    ).astype(jnp.bfloat16)
    tail = jnp.concatenate([tail_left, tail_right], axis=1) + dot(tail_att, wo[...]) + bias[...]
    tail = tail.astype(jnp.bfloat16).astype(jnp.float32)
    x[main_rows:, :] = layer_norm(tail, gain[...], tail_codes[...]).astype(jnp.bfloat16)
    q[...] = dot(x[...], wq[...]).astype(jnp.bfloat16)
    k[...] = dot(x[...], wk[...]).astype(jnp.bfloat16)
    v[...] = dot(x[...], wv[...]).astype(jnp.bfloat16)
    row = lax.broadcasted_iota(jnp.int32, (main_rows, main_rows), 0)
    col = lax.broadcasted_iota(jnp.int32, (main_rows, main_rows), 1)
    heads = masked_attention(
        q[:main_rows, :], k[:main_rows, :], v[:main_rows, :], (row & 15) == (col & 15)
    ).astype(jnp.bfloat16)
    out[:, : 2 * MAIN, :] = heads.reshape(8, 2 * MAIN, half)
    row = lax.broadcasted_iota(jnp.int32, (tail_rows, tail_rows), 0)
    col = lax.broadcasted_iota(jnp.int32, (tail_rows, tail_rows), 1)
    heads = masked_attention(
        q[main_rows:, :], k[main_rows:, :], v[main_rows:, :], ((row ^ col) & 5) == 0
    ).astype(jnp.bfloat16)
    out[:, 2 * MAIN :, :] = heads.reshape(8, 8, half)


def place_kernel(packed, out, tail):
    for d in range(8):
        for f in range(2):
            out[f, MAIN * d : MAIN * d + MAIN, :] = packed[d, MAIN * f : MAIN * f + MAIN, :]
        rest = packed[d, 2 * MAIN :, :].astype(jnp.float32)
        for f in range(2):
            tail[f, 2 * d : 2 * d + 2, :] = rest[2 * f : 2 * f + 2, :]
    for f in range(2):
        out[f, 8 * MAIN :, :] = tail[f].astype(jnp.bfloat16)


def body(
    latents,
    reference_features,
    norm_gain,
    query_weight,
    key_weight,
    value_weight,
    out_weight,
    out_bias,
    motion_gain,
    motion_query,
    motion_key,
    motion_value,
):
    frames, row_count, col_count, channels = latents.shape
    places = row_count * col_count
    width = query_weight.shape[1]
    bf16 = functools.partial(jax.ShapeDtypeStruct, dtype=jnp.bfloat16)
    f32 = functools.partial(jax.ShapeDtypeStruct, dtype=jnp.float32)
    lat = latents.reshape(frames, places, channels)
    gain = norm_gain.reshape(1, channels)
    bias = out_bias.reshape(1, channels)
    motion = motion_gain.reshape(1, channels)

    from_y = [send(lat[f], Y_FLIP) for f in range(2)]
    from_c = send(lat, C_FLIP)
    from_yc = [send(from_y[f], C_FLIP) for f in range(2)]

    own = reference_features
    tokens = jnp.concatenate(
        [own] + [send(own, pairs) for pairs in (C_FLIP, Y_FLIP, YC_FLIP)], axis=0
    )
    ring = [tokens]
    for _ in range(4):
        ring.append(send(ring[-1], Z_RING))
    other = send(jnp.stack(ring[1:4]), C_FLIP)
    token_parts = ring + [other[0], other[1], other[2]]

    packed_lat = call(
        pack_kernel,
        bf16((8, 72, width)),
        (lat,),
        scratch=[pltpu.VMEM((2, 16, channels), jnp.float32)],
        moved=1500000,
    )
    lat_cells = exchange(packed_lat)

    own_parts = []
    for f in range(2):
        pick = pl.BlockSpec((None, places, channels), lambda i, f=f: (f, 0, 0))
        args = (lat, from_c, from_y[f], from_yc[f], gain, query_weight, key_weight, value_weight)
        own_parts.append(
            call(
                own_kernel,
                (
                    bf16((places, width)),
                    f32((HEADS, places, 256)),
                    f32((places, 128)),
                ),
                args,
                in_specs=[pick, pick] + [whole(a) for a in args[2:]],
                scratch=[
                    pltpu.VMEM((4 * places, channels), jnp.bfloat16),
                    pltpu.VMEM((4 * places, width), jnp.bfloat16),
                    pltpu.VMEM((4 * places, width), jnp.bfloat16),
                ],
                flops=2700000000,
                moved=7000000,
            )
        )
    ref_k, ref_v = call(
        ref_kernel,
        (bf16((4 * places, width)), bf16((4 * places, width))),
        (*token_parts, key_weight, value_weight),
        flops=1900000000,
        moved=6000000,
    )
    att, packed_att = call(
        join_kernel,
        (bf16((2, places, width)), bf16((8, 40, width))),
        (*own_parts[0], *own_parts[1], ref_k, ref_v),
        scratch=[pltpu.VMEM((2, 16, width), jnp.float32)],
        flops=500000000,
        moved=4000000,
    )
    att_cells = exchange(packed_att)
    block = call(
        block_kernel,
        bf16((2, places, channels)),
        (lat, att, out_weight, bias),
        flops=500000000,
        moved=3500000,
    )
    codes = position_codes(channels)
    tail_codes = np.repeat(
        np.pad(codes.reshape(8, 2, channels), ((0, 0), (0, 2), (0, 0))), 2, axis=1
    ).reshape(64, channels)
    rows = 320
    heads = call(
        motion_kernel,
        bf16((8, 40, width)),
        (
            lat_cells,
            att_cells,
            out_weight,
            bias,
            motion,
            jnp.asarray(codes),
            jnp.asarray(tail_codes),
            motion_query,
            motion_key,
            motion_value,
        ),
        scratch=[
            pltpu.VMEM((rows, channels), jnp.bfloat16),
            pltpu.VMEM((rows, width), jnp.bfloat16),
            pltpu.VMEM((rows, width), jnp.bfloat16),
            pltpu.VMEM((rows, width), jnp.bfloat16),
        ],
        flops=2500000000,
        moved=9000000,
    )
    returned = exchange(heads)
    motion_heads = call(
        place_kernel,
        bf16((2, places, width)),
        (returned,),
        scratch=[pltpu.VMEM((2, 16, width), jnp.float32)],
        moved=800000,
    )
    return (
        block.reshape(frames, row_count, col_count, channels),
        motion_heads.reshape(frames, row_count, col_count, width),
    )


def solution(mesh):
    return jax.shard_map(
        body,
        mesh=mesh,
        in_specs=(P("tm", "rows", None, None), P(("tm", "rows"), None)) + (P(),) * 10,
        out_specs=(P("tm", "rows", None, None), P("tm", "rows", None, None)),
        check_vma=False,
    )
```

time: 388 us -> 118 us (0.30)
  waiting for transfers between devices: 249 us -> 44.6 us
  matrix products: 29.6 us -> 0 us
  local copies, waits for them, and re-layouts: 43.7 us -> 14.9 us
  Pallas kernels: 0 us -> 26.6 us
  between operations: 14.2 us -> 0.82 us
  other arithmetic: 13.4 us -> 0.96 us
  blocking collectives: 10.1 us -> 0 us
    ppermute x6 -> x13, waiting for transfers between devices: 216 us -> 16.5 us  [send(): return lax.ppermute(value, AXES, pairs)]
    all_gather x3 -> x0, waiting for transfers between devices: 33.5 us -> none  [the longest x1 20.5 us: body(): ref_pair = lax.all_gather(ref_pair, 'rows', axis=1, tiled=True)]
    all_to_all x0 -> x3, waiting for transfers between devices: none -> 28.1 us  [exchange(): lax.all_to_all(value, 'tm', 0, 0, axis_index_groups=shot_groups(), tiled=...]
    dot_general x14 -> x0, matrix products: 27.6 us -> none  [the longest x1 5.83 us: frame_attention(): jnp.einsum('fphd,gphd->phfg', query_heads, key_heads, preferred_element_t...]
    pallas_call x0 -> x8, Pallas kernels: none -> 26.6 us  [call(): pl.pallas_call(kernel, out_shape=out_shape, grid=(1,), in_specs=in_specs...]
    another operation x5 -> x0, local copies, waits for them, and re-layouts: 17.7 us -> none  [the longest x1 10.1 us: frame_attention(): key_heads = motion_k.reshape(motion_k.shape[0], cells, THEADS, THD)]
    all_to_all x0 -> x3, starting transfers between devices: none -> 13.3 us  [exchange(): lax.all_to_all(value, 'tm', 0, 0, axis_index_groups=shot_groups(), tiled=...]
    ppermute x6 -> x13, starting transfers between devices: 27.2 us -> 15.5 us  [send(): return lax.ppermute(value, AXES, pairs)]
  transfers between devices with their start and end apart: 9 -> 16, of which waited for: 8 -> 7; matrix products, arithmetic and copies ran while one was open for 6% -> 2% of each run, Pallas kernels for 0% -> 19%
where the time goes in v1:
time: 118 us; the launch traced here: 117 us
  waiting for transfers between devices  44.6 us (38%)
  starting transfers between devices  28.8 us (24%)
  Pallas kernels  26.6 us (23%)
  local copies, waits for them, and re-layouts  14.9 us (13%)
    all_to_all x3, waiting for transfers between devices, exchange(): lax.all_to_all(value, 'tm', 0, 0, axis_index_groups=shot_groups(), tiled=...  28.1 us
    pallas_call x8, Pallas kernels, call(): pl.pallas_call(kernel, out_shape=out_shape, grid=(1,), in_specs=in_specs...  26.6 us
    ppermute x13, waiting for transfers between devices, send(): return lax.ppermute(value, AXES, pairs)  16.5 us
    ppermute x13, starting transfers between devices, send(): return lax.ppermute(value, AXES, pairs)  15.5 us
    all_to_all x3, starting transfers between devices, exchange(): lax.all_to_all(value, 'tm', 0, 0, axis_index_groups=shot_groups(), tiled=...  13.3 us
    unnamed x36, local copies, waits for them, and re-layouts  12.9 us
  transfers between devices with their start and end apart: 16, of which 7 were waited for; matrix products, arithmetic and copies ran while one was open for 2% of the time, Pallas kernels for 19%

profile of v1, /device:TPU:2, one launch (start us, length us, event | category | flops | bytes accessed | tf_op | source)
XLA Modules:
  0.0 116.7 jit_solution(17085420511183090943)
XLA Ops:
  0.6 0.0 copy-start
  0.6 2.7 %collective-permute-start.7 = (bf16[18,1280]{1,0:T(8,128)(2,1)}, bf16[18,1280]{1,0:T(8,128)(2,1)S(1)}, u32[]{:S(2)}, u32[]{:S(2)}) collective-permute-start(bf16[18,1280]{1,0:T(8,128)(2,1)} %param.15), channel_id=1, source_target_pairs={{0,3},{1,2},{2,1},{3,0},{4,7},{5,6},{6,5},{7,4},{8,11},{9,10},{10,... | collective-permute-start | bytes 138248 | tf_op jit(solution)/shard_map/ppermute | solution.py:46
  3.4 0.7 collective-permute-start.6
  4.0 0.1 collective-permute-start.5
  4.1 0.4 collective-permute-start
  4.5 2.0 %collective-permute-done.7 = bf16[18,1280]{1,0:T(8,128)(2,1)S(1)} collective-permute-done((bf16[18,1280]{1,0:T(8,128)(2,1)}, bf16[18,1280]{1,0:T(8,128)(2,1)S(1)}, u32[]{:S(2)}, u32[]{:S(2)}) %collective-permute-start.7) | collective-permute-done | bytes 46112 | tf_op jit(solution)/shard_map/ppermute | solution.py:46
  6.5 3.2 %collective-permute-done.6 = bf16[18,1280]{1,0:T(8,128)(2,1)S(1)} collective-permute-done((bf16[18,1280]{1,0:T(8,128)(2,1)}, bf16[18,1280]{1,0:T(8,128)(2,1)S(1)}, u32[]{:S(2)}, u32[]{:S(2)}) %collective-permute-start.6) | collective-permute-done | bytes 46112 | tf_op jit(solution)/shard_map/ppermute | solution.py:46
  9.7 0.9 pad_maximum_fusion.1.t0
  10.6 2.0 %collective-permute-start.8 = (bf16[72,1280]{1,0:T(8,128)(2,1)S(1)}, bf16[72,1280]{1,0:T(8,128)(2,1)S(1)}, u32[]{:S(2)}, u32[]{:S(2)}) collective-permute-start(bf16[72,1280]{1,0:T(8,128)(2,1)S(1)} %pad_maximum_fusion.1.t0), channel_id=1, source_target_pairs={{0,4},{1,29},{2,6},{3,31},{4,8},{5,1},{6,10},{7,3},{8,12},{9,5},{1... | collective-permute-start | bytes 552968 | tf_op jit(solution)/shard_map/ppermute | solution.py:46
  12.6 1.9 %fusion = (bf16[1,6,24,1280]{3,2,1,0:T(8,128)(2,1)}, bf16[1,6,24,1280]{3,2,1,0:T(8,128)(2,1)S(1)}) fusion(bf16[2,6,24,1280]{3,2,1,0:T(8,128)(2,1)} %param.14), kind=kLoop, calls=%fused_computation.5 | loop fusion | bytes 1474560 | tf_op jit(solution)/shard_map/slice | solution.py:315
  14.4 1.6 %collective-permute-start.1 = (bf16[144,1280]{1,0:T(8,128)(2,1)S(1)}, bf16[144,1280]{1,0:T(8,128)(2,1)}, u32[]{:S(2)}, u32[]{:S(2)}) collective-permute-start(bf16[144,1280]{1,0:T(8,128)(2,1)S(1)} %bitcast.23), channel_id=1, source_target_pairs={{0,2},{1,3},{2,0},{3,1},{4,6},{5,7},{6,4},{7,5},{8,10},{9,11},{10,... | collective-permute-start | bytes 1105928 | tf_op jit(solution)/shard_map/ppermute | solution.py:46
  16.0 1.9 %collective-permute-start.3 = (bf16[144,1280]{1,0:T(8,128)(2,1)}, bf16[144,1280]{1,0:T(8,128)(2,1)S(1)}, u32[]{:S(2)}, u32[]{:S(2)}) collective-permute-start(bf16[144,1280]{1,0:T(8,128)(2,1)} %bitcast.2), channel_id=1, source_target_pairs={{0,2},{1,3},{2,0},{3,1},{4,6},{5,7},{6,4},{7,5},{8,10},{9,11},{10,... | collective-permute-start | bytes 1105928 | tf_op jit(solution)/shard_map/ppermute | solution.py:46
  18.0 2.0 %collective-permute-done.8.t1 = bf16[72,1280]{1,0:T(8,128)(2,1)S(1)} collective-permute-done((bf16[72,1280]{1,0:T(8,128)(2,1)S(1)}, bf16[72,1280]{1,0:T(8,128)(2,1)S(1)}, u32[]{:S(2)}, u32[]{:S(2)}) %collective-permute-start.8) | collective-permute-done | bytes 184352 | tf_op jit(solution)/shard_map/ppermute | solution.py:46
  20.0 6.7 %collective-permute-done.9.t2 = bf16[72,1280]{1,0:T(8,128)(2,1)S(1)} collective-permute-done((bf16[72,1280]{1,0:T(8,128)(2,1)S(1)}, bf16[72,1280]{1,0:T(8,128)(2,1)S(1)}, u32[]{:S(2)}, u32[]{:S(2)}) %collective-permute-start.9) | collective-permute-done | bytes 184352 | tf_op jit(solution)/shard_map/ppermute | solution.py:46
  26.8 3.3 %collective-permute-start.2 = (bf16[144,1280]{1,0:T(8,128)(2,1)}, bf16[144,1280]{1,0:T(8,128)(2,1)}, u32[]{:S(2)}, u32[]{:S(2)}) collective-permute-start(bf16[144,1280]{1,0:T(8,128)(2,1)} %collective-permute-done.1.peer_y), channel_id=1, source_target_pairs={{0,1},{1,0},{2,3},{3,2},{4,5},{5,4},{6,7},{7,6},{8,9},{9,8},{10,11... | collective-permute-start | bytes 1105928 | tf_op jit(solution)/shard_map/ppermute | solution.py:46
  30.1 1.0 shard_map.154
  31.1 5.2 %all-to-all-start = ((bf16[8,72,640]{2,1,0:T(8,128)(2,1)}), bf16[8,72,640]{2,1,0:T(8,128)(2,1)S(1)}, u32[]{:S(2)}, u32[]{:S(2)}) async-start(bf16[8,72,640]{2,1,0:T(8,128)(2,1)} %shard_map.154), calls=%async_computation | async-start | bytes 1474560 | tf_op jit(solution)/shard_map/all_to_all | solution.py:54
  36.3 0.3 collective-permute-start.4
  36.6 0.1 pad_maximum_fusion
  36.6 0.4 collective-permute-start.12
  37.0 2.1 %collective-permute-start.11 = (bf16[72,1280]{1,0:T(8,128)(2,1)S(1)}, bf16[72,1280]{1,0:T(8,128)(2,1)S(1)}, u32[]{:S(2)}, u32[]{:S(2)}) collective-permute-start(bf16[72,1280]{1,0:T(8,128)(2,1)S(1)} %collective-permute-done.10.t3), channel_id=1, source_target_pairs={{0,4},{1,29},{2,6},{3,31},{4,8},{5,1},{6,10},{7,3},{8,12},{9,5},{1... | collective-permute-start | bytes 552968 | tf_op jit(solution)/shard_map/ppermute | solution.py:46
  39.1 1.4 %copy-done.5 = bf16[1280,640]{1,0:T(8,128)(2,1)S(1)} copy-done((bf16[1280,640]{1,0:T(8,128)(2,1)S(1)}, bf16[1280,640]{1,0:T(8,128)(2,1)}, u32[]{:S(2)}) %copy-start.5) | copy-done | bytes 1638424
  40.5 1.4 %copy-done.7 = bf16[1280,640]{1,0:T(8,128)(2,1)S(1)} copy-done((bf16[1280,640]{1,0:T(8,128)(2,1)S(1)}, bf16[1280,640]{1,0:T(8,128)(2,1)}, u32[]{:S(2)}) %copy-start.7) | copy-done | bytes 1638424
  42.0 1.4 %copy-done.9 = bf16[1280,640]{1,0:T(8,128)(2,1)S(1)} copy-done((bf16[1280,640]{1,0:T(8,128)(2,1)S(1)}, bf16[1280,640]{1,0:T(8,128)(2,1)}, u32[]{:S(2)}) %copy-start.9) | copy-done | bytes 1638424
  43.4 6.6 %shard_map.149 = (bf16[144,640]{1,0:T(8,128)(2,1)S(1)}, f32[4,144,256]{2,1,0:T(8,128)S(1)}, f32[144,128]{1,0:T(8,128)S(1)}) custom-call(bf16[2,144,1280]{2,1,0:T(8,128)(2,1)S(1)} %bitcast.16, bf16[2,144,1280]{2,1,0:T(8,128)(2,1)S(1)} %collective-permute-done.peer_c, bf16[144,1280]{1,0:T(8,128)(2,1)} %collective-permute-done.1.peer_y, ...), custom_call_target="tpu_custom_call" | custom-call | flops 2700000000 | bytes 7000000 | tf_op jit(solution)/shard_map/pallas_call | solution.py:67
  50.0 0.0 copy-start.8
  50.1 5.4 %shard_map.150 = (bf16[144,640]{1,0:T(8,128)(2,1)S(1)}, f32[4,144,256]{2,1,0:T(8,128)S(1)}, f32[144,128]{1,0:T(8,128)S(1)}) custom-call(bf16[2,144,1280]{2,1,0:T(8,128)(2,1)S(1)} %bitcast.17, bf16[2,144,1280]{2,1,0:T(8,128)(2,1)S(1)} %collective-permute-done.peer_c, bf16[144,1280]{1,0:T(8,128)(2,1)S(1)} %collective-permute-done.3.peer_y, ...), custom_call_target="tpu_custom_call" | custom-call | flops 2700000000 | bytes 7000000 | tf_op jit(solution)/shard_map/pallas_call | solution.py:67
  55.5 2.6 %collective-permute-done.11.t4 = bf16[72,1280]{1,0:T(8,128)(2,1)S(1)} collective-permute-done((bf16[72,1280]{1,0:T(8,128)(2,1)S(1)}, bf16[72,1280]{1,0:T(8,128)(2,1)S(1)}, u32[]{:S(2)}, u32[]{:S(2)}) %collective-permute-start.11) | collective-permute-done | bytes 184352 | tf_op jit(solution)/shard_map/ppermute | solution.py:46
  58.1 2.5 %shard_map.151 = (bf16[576,640]{1,0:T(8,128)(2,1)S(1)}, bf16[576,640]{1,0:T(8,128)(2,1)S(1)}) custom-call(bf16[72,1280]{1,0:T(8,128)(2,1)S(1)} %pad_maximum_fusion.1.t0, bf16[72,1280]{1,0:T(8,128)(2,1)S(1)} %collective-permute-done.8.t1, bf16[72,1280]{1,0:T(8,128)(2,1)S(1)} %collective-permute-done.9.t2, bf16[72,1280]{1,0:T(8,128)(2,1)S(1)} %collective-permute-done.10.t3, ...), custom_call_target="tpu_custom_call" | custom-call | flops 1900000000 | bytes 6000000 | tf_op jit(solution)/shard_map/pallas_call | solution.py:67
  60.6 0.0 copy-start.17
  60.6 0.0 copy-start.1
  60.6 4.7 %shard_map.152 = (bf16[2,144,640]{2,1,0:T(8,128)(2,1)S(1)}, bf16[8,40,640]{2,1,0:T(8,128)(2,1)}) custom-call(bf16[144,640]{1,0:T(8,128)(2,1)S(1)} %get-tuple-element.12.q0, f32[4,144,256]{2,1,0:T(8,128)S(1)} %get-tuple-element.13.o0, f32[144,128]{1,0:T(8,128)S(1)} %get-tuple-element.14.ml0, bf16[144,640]{1,0:T(8,128)(2,1)S(1)} %get-tuple-element.15.q1, ...), custom_call_target="tpu_custom_call" | custom-call | flops 500000000 | bytes 4000000 | tf_op jit(solution)/shard_map/pallas_call | solution.py:67
  65.4 0.7 copy-done.3
  66.1 4.7 %all-to-all-start.1 = ((bf16[8,40,640]{2,1,0:T(8,128)(2,1)}), bf16[8,40,640]{2,1,0:T(8,128)(2,1)S(1)}, u32[]{:S(2)}, u32[]{:S(2)}) async-start(bf16[8,40,640]{2,1,0:T(8,128)(2,1)} %get-tuple-element.21), calls=%async_computation.1 | async-start | bytes 819200 | tf_op jit(solution)/shard_map/all_to_all | solution.py:54
  70.8 15.3 %all-to-all-done.1.att = bf16[8,40,640]{2,1,0:T(8,128)(2,1)S(1)} async-done(((bf16[8,40,640]{2,1,0:T(8,128)(2,1)}), bf16[8,40,640]{2,1,0:T(8,128)(2,1)S(1)}, u32[]{:S(2)}, u32[]{:S(2)}) %all-to-all-start.1) | async-done | bytes 409632 | tf_op jit(solution)/shard_map/all_to_all | solution.py:54
  86.1 1.4 %copy-done.10 = bf16[1280,640]{1,0:T(8,128)(2,1)S(1)} copy-done((bf16[1280,640]{1,0:T(8,128)(2,1)S(1)}, bf16[1280,640]{1,0:T(8,128)(2,1)}, u32[]{:S(2)}) %copy-start.10) | copy-done | bytes 1638424
  87.5 1.4 %copy-done.11 = bf16[1280,640]{1,0:T(8,128)(2,1)S(1)} copy-done((bf16[1280,640]{1,0:T(8,128)(2,1)S(1)}, bf16[1280,640]{1,0:T(8,128)(2,1)}, u32[]{:S(2)}) %copy-start.11) | copy-done | bytes 1638424
  89.0 1.4 %copy-done.12 = bf16[1280,640]{1,0:T(8,128)(2,1)S(1)} copy-done((bf16[1280,640]{1,0:T(8,128)(2,1)S(1)}, bf16[1280,640]{1,0:T(8,128)(2,1)}, u32[]{:S(2)}) %copy-start.12) | copy-done | bytes 1638424
  90.4 1.0 copy-done.13
  91.4 0.9 copy-done.14
  92.3 4.0 %shard_map.155 = bf16[8,40,640]{2,1,0:T(8,128)(2,1)S(1)} custom-call(bf16[8,72,640]{2,1,0:T(8,128)(2,1)S(1)} %all-to-all-done.lat, bf16[8,40,640]{2,1,0:T(8,128)(2,1)S(1)} %all-to-all-done.1.att, bf16[640,1280]{1,0:T(8,128)(2,1)S(1)} %copy-done.1, f32[1,1280]{1,0:T(1,128)S(1)} %reshape.28.bias, f32[1,1280]{1,0:T(1,128)S(1)} %reshape.30.gain, ...), custom_call_target="tpu_custom_call" | custom-call | flops 2500000000 | bytes 9000000 | tf_op jit(solution)/shard_map/pallas_call | solution.py:67
  96.3 0.7 copy-done.2
  97.0 3.5 %all-to-all-start.2 = ((bf16[8,40,640]{2,1,0:T(8,128)(2,1)}), bf16[8,40,640]{2,1,0:T(8,128)(2,1)S(1)}, u32[]{:S(2)}, u32[]{:S(2)}) async-start(bf16[8,40,640]{2,1,0:T(8,128)(2,1)} %copy-done.2), calls=%async_computation.2 | async-start | bytes 819200 | tf_op jit(solution)/shard_map/all_to_all | solution.py:54
  100.5 0.0 copy-start.4
  100.5 1.0 copy-done.4
  101.5 1.6 %shard_map.153 = bf16[2,144,1280]{2,1,0:T(8,128)(2,1)} custom-call(bf16[2,144,1280]{2,1,0:T(8,128)(2,1)S(1)} %bitcast.18, bf16[2,144,640]{2,1,0:T(8,128)(2,1)S(1)} %copy-done.4, bf16[640,1280]{1,0:T(8,128)(2,1)S(1)} %copy-done.1, f32[1,1280]{1,0:T(1,128)S(1)} %reshape.28.bias), custom_call_target="tpu_custom_call" | custom-call | flops 500000000 | bytes 3500000 | tf_op jit(solution)/shard_map/pallas_call | solution.py:67
  103.1 12.8 %all-to-all-done.2.packed = bf16[8,40,640]{2,1,0:T(8,128)(2,1)S(1)} async-done(((bf16[8,40,640]{2,1,0:T(8,128)(2,1)}), bf16[8,40,640]{2,1,0:T(8,128)(2,1)S(1)}, u32[]{:S(2)}, u32[]{:S(2)}) %all-to-all-start.2) | async-done | bytes 409632 | tf_op jit(solution)/shard_map/all_to_all | solution.py:54
  115.9 0.8 shard_map.156
  (35 shorter events, 0.1 us)
Async XLA Ops:
  0.6 29.5 %copy-start = (bf16[2,6,24,1280]{3,2,1,0:T(8,128)(2,1)S(1)}, bf16[2,6,24,1280]{3,2,1,0:T(8,128)(2,1)}, u32[]{:S(2)}) copy-start(bf16[2,6,24,1280]{3,2,1,0:T(8,128)(2,1)} %param.14) | copy-start | bytes 2211844
  0.6 5.9 %collective-permute-start.7 = (bf16[18,1280]{1,0:T(8,128)(2,1)}, bf16[18,1280]{1,0:T(8,128)(2,1)S(1)}, u32[]{:S(2)}, u32[]{:S(2)}) collective-permute-start(bf16[18,1280]{1,0:T(8,128)(2,1)} %param.15), channel_id=1, source_target_pairs={{0,3},{1,2},{2,1},{3,0},{4,7},{5,6},{6,5},{7,4},{8,11},{9,10},{10,... | collective-permute-start | bytes 138248 | tf_op jit(solution)/shard_map/ppermute | solution.py:46
  3.4 6.3 %collective-permute-start.6 = (bf16[18,1280]{1,0:T(8,128)(2,1)}, bf16[18,1280]{1,0:T(8,128)(2,1)S(1)}, u32[]{:S(2)}, u32[]{:S(2)}) collective-permute-start(bf16[18,1280]{1,0:T(8,128)(2,1)} %param.15), channel_id=1, source_target_pairs={{0,2},{1,3},{2,0},{3,1},{4,6},{5,7},{6,4},{7,5},{8,10},{9,11},{10,... | collective-permute-start | bytes 138248 | tf_op jit(solution)/shard_map/ppermute | solution.py:46
  4.0 5.6 %collective-permute-start.5 = (bf16[18,1280]{1,0:T(8,128)(2,1)}, bf16[18,1280]{1,0:T(8,128)(2,1)S(1)}, u32[]{:S(2)}, u32[]{:S(2)}) collective-permute-start(bf16[18,1280]{1,0:T(8,128)(2,1)} %param.15), channel_id=1, source_target_pairs={{0,1},{1,0},{2,3},{3,2},{4,5},{5,4},{6,7},{7,6},{8,9},{9,8},{10,11... | collective-permute-start | bytes 138248 | tf_op jit(solution)/shard_map/ppermute | solution.py:46
  4.1 35.0 %collective-permute-start = (bf16[2,144,1280]{2,1,0:T(8,128)(2,1)}, bf16[2,144,1280]{2,1,0:T(8,128)(2,1)S(1)}, u32[]{:S(2)}, u32[]{:S(2)}) collective-permute-start(bf16[2,144,1280]{2,1,0:T(8,128)(2,1)} %bitcast.14), channel_id=1, source_target_pairs={{0,1},{1,0},{2,3},{3,2},{4,5},{5,4},{6,7},{7,6},{8,9},{9,8},{10,11... | collective-permute-start | bytes 2211848 | tf_op jit(solution)/shard_map/ppermute | solution.py:46
  10.6 9.5 %collective-permute-start.8 = (bf16[72,1280]{1,0:T(8,128)(2,1)S(1)}, bf16[72,1280]{1,0:T(8,128)(2,1)S(1)}, u32[]{:S(2)}, u32[]{:S(2)}) collective-permute-start(bf16[72,1280]{1,0:T(8,128)(2,1)S(1)} %pad_maximum_fusion.1.t0), channel_id=1, source_target_pairs={{0,4},{1,29},{2,6},{3,31},{4,8},{5,1},{6,10},{7,3},{8,12},{9,5},{1... | collective-permute-start | bytes 552968 | tf_op jit(solution)/shard_map/ppermute | solution.py:46
  14.4 12.3 %collective-permute-start.1 = (bf16[144,1280]{1,0:T(8,128)(2,1)S(1)}, bf16[144,1280]{1,0:T(8,128)(2,1)}, u32[]{:S(2)}, u32[]{:S(2)}) collective-permute-start(bf16[144,1280]{1,0:T(8,128)(2,1)S(1)} %bitcast.23), channel_id=1, source_target_pairs={{0,2},{1,3},{2,0},{3,1},{4,6},{5,7},{6,4},{7,5},{8,10},{9,11},{10,... | collective-permute-start | bytes 1105928 | tf_op jit(solution)/shard_map/ppermute | solution.py:46
  16.0 20.2 %collective-permute-start.3 = (bf16[144,1280]{1,0:T(8,128)(2,1)}, bf16[144,1280]{1,0:T(8,128)(2,1)S(1)}, u32[]{:S(2)}, u32[]{:S(2)}) collective-permute-start(bf16[144,1280]{1,0:T(8,128)(2,1)} %bitcast.2), channel_id=1, source_target_pairs={{0,2},{1,3},{2,0},{3,1},{4,6},{5,7},{6,4},{7,5},{8,10},{9,11},{10,... | collective-permute-start | bytes 1105928 | tf_op jit(solution)/shard_map/ppermute | solution.py:46
  20.0 6.7 %collective-permute-start.9 = (bf16[72,1280]{1,0:T(8,128)(2,1)S(1)}, bf16[72,1280]{1,0:T(8,128)(2,1)S(1)}, u32[]{:S(2)}, u32[]{:S(2)}) collective-permute-start(bf16[72,1280]{1,0:T(8,128)(2,1)S(1)} %collective-permute-done.8.t1), channel_id=1, source_target_pairs={{0,4},{1,29},{2,6},{3,31},{4,8},{5,1},{6,10},{7,3},{8,12},{9,5},{1... | collective-permute-start | bytes 552968 | tf_op jit(solution)/shard_map/ppermute | solution.py:46
  26.8 9.8 %collective-permute-start.10 = (bf16[72,1280]{1,0:T(8,128)(2,1)S(1)}, bf16[72,1280]{1,0:T(8,128)(2,1)S(1)}, u32[]{:S(2)}, u32[]{:S(2)}) collective-permute-start(bf16[72,1280]{1,0:T(8,128)(2,1)S(1)} %collective-permute-done.9.t2), channel_id=1, source_target_pairs={{0,4},{1,29},{2,6},{3,31},{4,8},{5,1},{6,10},{7,3},{8,12},{9,5},{1... | collective-permute-start | bytes 552968 | tf_op jit(solution)/shard_map/ppermute | solution.py:46
  26.8 12.3 %collective-permute-start.2 = (bf16[144,1280]{1,0:T(8,128)(2,1)}, bf16[144,1280]{1,0:T(8,128)(2,1)}, u32[]{:S(2)}, u32[]{:S(2)}) collective-permute-start(bf16[144,1280]{1,0:T(8,128)(2,1)} %collective-permute-done.1.peer_y), channel_id=1, source_target_pairs={{0,1},{1,0},{2,3},{3,2},{4,5},{5,4},{6,7},{7,6},{8,9},{9,8},{10,11... | collective-permute-start | bytes 1105928 | tf_op jit(solution)/shard_map/ppermute | solution.py:46
  31.1 6.0 %copy-start.15 = (f32[1280]{0:T(1024)S(1)}, f32[1280]{0:T(1024)}, u32[]{:S(2)}) copy-start(f32[1280]{0:T(1024)} %param.16) | copy-start | bytes 15364
  31.1 35.0 %all-to-all-start = ((bf16[8,72,640]{2,1,0:T(8,128)(2,1)}), bf16[8,72,640]{2,1,0:T(8,128)(2,1)S(1)}, u32[]{:S(2)}, u32[]{:S(2)}) async-start(bf16[8,72,640]{2,1,0:T(8,128)(2,1)} %shard_map.154), calls=%async_computation | async-start | bytes 1474560 | tf_op jit(solution)/shard_map/all_to_all | solution.py:54
  36.3 13.8 %collective-permute-start.4 = (bf16[144,1280]{1,0:T(8,128)(2,1)S(1)}, bf16[144,1280]{1,0:T(8,128)(2,1)S(1)}, u32[]{:S(2)}, u32[]{:S(2)}) collective-permute-start(bf16[144,1280]{1,0:T(8,128)(2,1)S(1)} %collective-permute-done.3.peer_y), channel_id=1, source_target_pairs={{0,1},{1,0},{2,3},{3,2},{4,5},{5,4},{6,7},{7,6},{8,9},{9,8},{10,11... | collective-permute-start | bytes 1105928 | tf_op jit(solution)/shard_map/ppermute | solution.py:46
  36.6 18.8 %collective-permute-start.12 = (bf16[3,72,1280]{2,1,0:T(8,128)(2,1)S(1)}, bf16[3,72,1280]{2,1,0:T(8,128)(2,1)S(1)}, u32[]{:S(2)}, u32[]{:S(2)}) collective-permute-start(bf16[3,72,1280]{2,1,0:T(8,128)(2,1)S(1)} %pad_maximum_fusion), channel_id=1, source_target_pairs={{0,1},{1,0},{2,3},{3,2},{4,5},{5,4},{6,7},{7,6},{8,9},{9,8},{10,11... | collective-permute-start | bytes 1658888 | tf_op jit(solution)/shard_map/ppermute | solution.py:46
  37.0 21.1 %collective-permute-start.11 = (bf16[72,1280]{1,0:T(8,128)(2,1)S(1)}, bf16[72,1280]{1,0:T(8,128)(2,1)S(1)}, u32[]{:S(2)}, u32[]{:S(2)}) collective-permute-start(bf16[72,1280]{1,0:T(8,128)(2,1)S(1)} %collective-permute-done.10.t3), channel_id=1, source_target_pairs={{0,4},{1,29},{2,6},{3,31},{4,8},{5,1},{6,10},{7,3},{8,12},{9,5},{1... | collective-permute-start | bytes 552968 | tf_op jit(solution)/shard_map/ppermute | solution.py:46
  39.1 1.4 %copy-start.5 = (bf16[1280,640]{1,0:T(8,128)(2,1)S(1)}, bf16[1280,640]{1,0:T(8,128)(2,1)}, u32[]{:S(2)}) copy-start(bf16[1280,640]{1,0:T(8,128)(2,1)} %wq.4) | copy-start | bytes 4915204
  40.5 1.4 %copy-start.7 = (bf16[1280,640]{1,0:T(8,128)(2,1)S(1)}, bf16[1280,640]{1,0:T(8,128)(2,1)}, u32[]{:S(2)}) copy-start(bf16[1280,640]{1,0:T(8,128)(2,1)} %wk.6) | copy-start | bytes 4915204
  42.0 1.4 %copy-start.9 = (bf16[1280,640]{1,0:T(8,128)(2,1)S(1)}, bf16[1280,640]{1,0:T(8,128)(2,1)}, u32[]{:S(2)}) copy-start(bf16[1280,640]{1,0:T(8,128)(2,1)} %wv.6) | copy-start | bytes 4915204
  43.4 6.7 %copy-start.6 = (bf16[1280,640]{1,0:T(8,128)(2,1)S(1)}, bf16[1280,640]{1,0:T(8,128)(2,1)}, u32[]{:S(2)}) copy-start(bf16[1280,640]{1,0:T(8,128)(2,1)} %wq.4) | copy-start | bytes 4915204
  50.0 8.1 %copy-start.8 = (bf16[1280,640]{1,0:T(8,128)(2,1)S(1)}, bf16[1280,640]{1,0:T(8,128)(2,1)}, u32[]{:S(2)}) copy-start(bf16[1280,640]{1,0:T(8,128)(2,1)} %wk.6) | copy-start | bytes 4915204
  60.6 10.2 %copy-start.16 = (f32[1280]{0:T(1024)S(1)}, f32[1280]{0:T(1024)}, u32[]{:S(2)}) copy-start(f32[1280]{0:T(1024)} %param.21) | copy-start | bytes 15364
  60.6 10.2 %copy-start.17 = (f32[1280]{0:T(1024)S(1)}, f32[1280]{0:T(1024)}, u32[]{:S(2)}) copy-start(f32[1280]{0:T(1024)} %param.22) | copy-start | bytes 15364
  60.6 25.5 %copy-start.1 = (bf16[640,1280]{1,0:T(8,128)(2,1)S(1)}, bf16[640,1280]{1,0:T(8,128)(2,1)}, u32[]{:S(2)}) copy-start(bf16[640,1280]{1,0:T(8,128)(2,1)} %wo.3) | copy-start | bytes 4915204
  65.4 0.7 copy-start.3
  66.1 20.0 %all-to-all-start.1 = ((bf16[8,40,640]{2,1,0:T(8,128)(2,1)}), bf16[8,40,640]{2,1,0:T(8,128)(2,1)S(1)}, u32[]{:S(2)}, u32[]{:S(2)}) async-start(bf16[8,40,640]{2,1,0:T(8,128)(2,1)} %get-tuple-element.21), calls=%async_computation.1 | async-start | bytes 819200 | tf_op jit(solution)/shard_map/all_to_all | solution.py:54
  86.1 1.4 %copy-start.10 = (bf16[1280,640]{1,0:T(8,128)(2,1)S(1)}, bf16[1280,640]{1,0:T(8,128)(2,1)}, u32[]{:S(2)}) copy-start(bf16[1280,640]{1,0:T(8,128)(2,1)} %wq.5) | copy-start | bytes 4915204
  87.5 1.4 %copy-start.11 = (bf16[1280,640]{1,0:T(8,128)(2,1)S(1)}, bf16[1280,640]{1,0:T(8,128)(2,1)}, u32[]{:S(2)}) copy-start(bf16[1280,640]{1,0:T(8,128)(2,1)} %wk.7) | copy-start | bytes 4915204
  89.0 1.4 %copy-start.12 = (bf16[1280,640]{1,0:T(8,128)(2,1)S(1)}, bf16[1280,640]{1,0:T(8,128)(2,1)}, u32[]{:S(2)}) copy-start(bf16[1280,640]{1,0:T(8,128)(2,1)} %wv.7) | copy-start | bytes 4915204
  90.4 1.0 copy-start.13
  91.4 0.9 copy-start.14
  96.3 0.7 copy-start.2
  97.0 18.9 %all-to-all-start.2 = ((bf16[8,40,640]{2,1,0:T(8,128)(2,1)}), bf16[8,40,640]{2,1,0:T(8,128)(2,1)S(1)}, u32[]{:S(2)}, u32[]{:S(2)}) async-start(bf16[8,40,640]{2,1,0:T(8,128)(2,1)} %copy-done.2), calls=%async_computation.2 | async-start | bytes 819200 | tf_op jit(solution)/shard_map/all_to_all | solution.py:54
  100.5 1.0 copy-start.4

commit v2 on v1

v2 whole, which is shorter than its diff:
```python
import functools
import math

import jax
import jax.numpy as jnp
import numpy as np
from jax import lax
from jax.experimental import pallas as pl
from jax.experimental.pallas import tpu as pltpu
from jax.sharding import PartitionSpec as P

GROUPS = 32
HEADS = 4
HD = 160
SHOT = 16
WINDOWS = tuple(HD * h // 128 * 128 for h in range(HEADS))
SCALE = math.log2(math.e) / math.sqrt(HD)
AXES = ("tm", "rows")
MAIN = 16
NT = (((1,), (1,)), ((), ()))
VMEM = 20 * 1024 * 1024


def mesh_perm(move):
    def flat(yl, x, z, yh, c):
        return ((yl * 4 + x) * 8 + z) * 4 + yh * 2 + c

    places = [
        (yl, x, z, yh, c)
        for yl in range(2)
        for x in range(4)
        for z in range(8)
        for yh in range(2)
        for c in range(2)
    ]
    return [(flat(*p), flat(*move(*p))) for p in places]


Y_FLIP = mesh_perm(lambda yl, x, z, yh, c: (yl, x, z, 1 - yh, c))
C_FLIP = mesh_perm(lambda yl, x, z, yh, c: (yl, x, z, yh, 1 - c))


def z_perm(step):
    return mesh_perm(
        lambda yl, x, z, yh, c: (yl, x, (z + (step if c == 0 else 8 - step)) % 8, yh, c)
    )


def send(value, pairs):
    return lax.ppermute(value, AXES, pairs)


def shot_groups():
    return [list(range(8 * g, 8 * g + 8)) for g in range(8)]


def exchange(value):
    return lax.all_to_all(value, "tm", 0, 0, axis_index_groups=shot_groups(), tiled=True)


def position_codes(channels):
    halves = np.arange(channels // 2, dtype=np.float64)
    rates = np.exp(-math.log(10000.0) * 2.0 * halves / channels)
    angles = np.arange(SHOT, dtype=np.float64)[:, None] * rates[None, :]
    return np.stack([np.sin(angles), np.cos(angles)], axis=-1).reshape(SHOT, channels).astype(
        np.float32
    )


def call(
    kernel, out_shape, args, in_specs=None, out_specs=None, scratch=(), flops=0, moved=0
):
    return pl.pallas_call(
        kernel,
        out_shape=out_shape,
        grid=(1,),
        in_specs=in_specs or [whole(a) for a in args],
        out_specs=out_specs or jax.tree.map(whole, out_shape),
        scratch_shapes=scratch,
        compiler_params=pltpu.CompilerParams(vmem_limit_bytes=VMEM),
        cost_estimate=pl.CostEstimate(flops=flops, bytes_accessed=moved, transcendentals=0),
    )(*args)


def whole(a):
    rank = len(a.shape)
    return pl.BlockSpec(a.shape, lambda i: (0,) * rank)


def head_window(x, h):
    w = WINDOWS[h]
    part = x[:, w : w + 256]
    lane = lax.broadcasted_iota(jnp.int32, part.shape, 1)
    low = HD * h - w
    return jnp.where((lane >= low) & (lane < low + HD), part, jnp.zeros_like(part))


def side_by_side(parts):
    lane = lax.broadcasted_iota(jnp.int32, (parts[0].shape[0], 128), 1)
    cols = [parts[0][:, :128]]
    for h in range(1, HEADS):
        edge = HD * h - WINDOWS[h]
        cols.append(jnp.where(lane < edge, parts[h - 1][:, 128:], parts[h][:, :128]))
    cols.append(parts[HEADS - 1][:, 128:])
    return jnp.concatenate(cols, axis=1)


def dot(a, b):
    return jnp.dot(a, b, preferred_element_type=jnp.float32)


def split_rows(x):
    high = x.astype(jnp.bfloat16).astype(jnp.float32)
    middle = (x - high).astype(jnp.bfloat16).astype(jnp.float32)
    return jnp.concatenate([high, middle, x - high - middle], axis=0).astype(jnp.bfloat16)


def join_rows(x):
    return x[0:8] + x[8:16] + x[16:24]


def group_stats(sums, count):
    channels = sums.shape[1]
    width = channels // GROUPS
    ch = lax.broadcasted_iota(jnp.int32, (channels, 128), 0)
    gr = lax.broadcasted_iota(jnp.int32, (channels, 128), 1) * width
    member = jnp.where((ch >= gr) & (ch < gr + width), 1.0, 0.0).astype(jnp.bfloat16)
    zeros = jnp.zeros((4, channels), jnp.float32)
    grouped = join_rows(dot(split_rows(jnp.concatenate([sums, zeros], axis=0)), member)) / count
    mean = grouped[0:2]
    rstd = lax.rsqrt(grouped[2:4] - mean * mean + 1e-05)
    both = jnp.concatenate([mean, rstd, jnp.zeros((4, 128), jnp.float32)], axis=0)
    return join_rows(
        lax.dot_general(split_rows(both), member, NT, preferred_element_type=jnp.float32)
    )


def own_kernel(
    lat, peer_c, peer_y, peer_yc, gain, wkv, wq, q_out, o_out, ml_out, xn, kv
):
    _, places, channels = lat.shape
    width = channels // 2
    everyone = (lat, peer_c, peer_y, peer_yc)
    cells = len(everyone) * places
    sums, squares = [], []
    for f in range(2):
        s1 = jnp.zeros((1, channels), jnp.float32)
        s2 = jnp.zeros((1, channels), jnp.float32)
        for piece in everyone:
            x = piece[f].astype(jnp.float32)
            s1 += jnp.sum(x, axis=0, keepdims=True)
            s2 += jnp.sum(x * x, axis=0, keepdims=True)
        sums.append(s1)
        squares.append(s2)
    stats = group_stats(jnp.concatenate(sums + squares, axis=0), cells * (channels // GROUPS))
    for f in range(2):
        mean = stats[f : f + 1]
        scale = stats[2 + f : 3 + f] * gain[...]
        for i, piece in enumerate(everyone):
            at = f * cells + i * places
            x = (piece[f].astype(jnp.float32) - mean) * scale
            xn[at : at + places, :] = x.astype(jnp.bfloat16)
    kv[...] = dot(xn[...], wkv[...]).astype(jnp.bfloat16)
    lane = lax.broadcasted_iota(jnp.int32, (places, 128), 1)
    for f in range(2):
        mine = slice(f * places, (f + 1) * places)
        keys = slice(f * cells, (f + 1) * cells)
        q = dot(xn[f * cells : f * cells + places, :], wq[...]).astype(jnp.bfloat16)
        q_out[mine, :] = q
        ml = jnp.zeros((places, 128), jnp.float32)
        for h in range(HEADS):
            w = WINDOWS[h]
            s = lax.dot_general(
                head_window(q, h), kv[keys, w : w + 256], NT, preferred_element_type=jnp.float32
            )
            top = jnp.max(s, axis=1, keepdims=True)
            p = jnp.exp2((s - top) * SCALE)
            total = jnp.sum(p, axis=1, keepdims=True)
            o_out[h, mine, :] = dot(p.astype(jnp.bfloat16), kv[keys, width + w : width + w + 256])
            ml = jnp.where(lane == h, top, jnp.where(lane == HEADS + h, total, ml))
        ml_out[mine, :] = ml


def tokens_kernel(own, far, near1, near2, near3, flag, out, rows):
    at = 0
    for part in (own, far, near1, near2, near3):
        rows[at : at + part.shape[0], :] = part[...].astype(jnp.float32)
        at += part.shape[0]
    out[...] = rows[...].astype(jnp.bfloat16)


def join_kernel(
    t0, t1, t2, t3, q, o, ml, lat, bias, gain, codes, wkv, wo, att_out, packed, tokens, kv, tail
):
    places, channels = t0.shape
    width = channels // 2
    for i, t in enumerate((t0, t1, t2, t3)):
        tokens[places * i : places * (i + 1), :] = t[...]
    kv[...] = dot(tokens[...], wkv[...]).astype(jnp.bfloat16)
    parts = []
    for h in range(HEADS):
        w = WINDOWS[h]
        s = lax.dot_general(
            head_window(q[...], h), kv[:, w : w + 256], NT, preferred_element_type=jnp.float32
        )
        before = ml[:, h : h + 1]
        top = jnp.maximum(before, jnp.max(s, axis=1, keepdims=True))
        p = jnp.exp2((s - top) * SCALE)
        keep = jnp.exp2((before - top) * SCALE)
        total = ml[:, HEADS + h : HEADS + h + 1] * keep + jnp.sum(p, axis=1, keepdims=True)
        mixed = o[h] * keep + dot(p.astype(jnp.bfloat16), kv[:, width + w : width + w + 256])
        parts.append(mixed * (1.0 / total))
    att_out[...] = side_by_side(parts).astype(jnp.bfloat16)
    for f in range(2):
        mine = slice(f * places, (f + 1) * places)
        block = lat[f].astype(jnp.float32) + dot(att_out[mine, :], wo[...]) + bias[...]
        block = block.astype(jnp.bfloat16).astype(jnp.float32)
        moving = layer_norm(block, gain[...], codes[f : f + 1, :])
        tail[f] = moving[8 * MAIN :, :]
        moving = moving.astype(jnp.bfloat16)
        for s in range(2):
            for d in range(8):
                at = 2 * MAIN * s + MAIN * f
                packed[d, at : at + MAIN, :] = moving[
                    MAIN * d : MAIN * d + MAIN, width * s : width * s + width
                ]
    for d in range(8):
        rows = [
            tail[f, 2 * d : 2 * d + 2, width * s : width * s + width]
            for s in range(2)
            for f in range(2)
        ]
        packed[d, 4 * MAIN :, :] = jnp.concatenate(rows, axis=0).astype(jnp.bfloat16)


def load(pairs, sems):
    copies = [
        pltpu.make_async_copy(source, target, sems.at[i])
        for i, (source, target) in enumerate(pairs)
    ]
    for copy in copies:
        copy.start()
    return copies


def weights_kernel(wk, wv, wq, wo, mq, mk, mv, wkv, wq_out, wo_out, mqkv, flag, sems):
    width = wk.shape[1]
    copies = load(
        (
            (wk, wkv.at[:, :width]),
            (wv, wkv.at[:, width:]),
            (wq, wq_out),
            (wo, wo_out),
            (mq, mqkv.at[:, :width]),
            (mk, mqkv.at[:, width : 2 * width]),
            (mv, mqkv.at[:, 2 * width :]),
        ),
        sems,
    )
    flag[...] = jnp.zeros_like(flag)
    for copy in copies:
        copy.wait()


def block_kernel(lat, att, bias, wo, after, out):
    places = lat.shape[1]
    for f in range(2):
        mine = slice(f * places, (f + 1) * places)
        out[f] = (
            lat[f].astype(jnp.float32) + dot(att[mine, :], wo[...]) + bias[...]
        ).astype(jnp.bfloat16)


def layer_norm(x, gain, codes):
    mean = jnp.mean(x, axis=-1, keepdims=True)
    centered = x - mean
    var = jnp.mean(centered * centered, axis=-1, keepdims=True)
    return centered * lax.rsqrt(var + 1e-05) * gain + codes


def masked_attention(qkv, rows, same):
    width = qkv.shape[1] // 3
    q = qkv[rows, :width]
    parts = []
    for h in range(HEADS):
        w = WINDOWS[h]
        s = lax.dot_general(
            head_window(q, h),
            qkv[rows, width + w : width + w + 256],
            NT,
            preferred_element_type=jnp.float32,
        )
        s = jnp.where(same, s, -jnp.inf)
        top = jnp.max(s, axis=1, keepdims=True)
        p = jnp.exp2((s - top) * SCALE)
        total = jnp.sum(p, axis=1, keepdims=True)
        values = qkv[rows, 2 * width + w : 2 * width + w + 256]
        parts.append(dot(p.astype(jnp.bfloat16), values) * (1.0 / total))
    return side_by_side(parts)


def motion_kernel(moving, weights, out, x, qkv):
    half = moving.shape[2]
    main_rows = 8 * 2 * MAIN
    tail_rows = 64
    x[:main_rows, :half] = moving[:, : 2 * MAIN, :].reshape(main_rows, half)
    x[:main_rows, half:] = moving[:, 2 * MAIN : 4 * MAIN, :].reshape(main_rows, half)
    tail = moving[:, 4 * MAIN :, :].reshape(tail_rows, half)
    x[main_rows:, :half] = tail
    x[main_rows:, half:] = pltpu.roll(tail.astype(jnp.float32), tail_rows - 4, 0).astype(
        jnp.bfloat16
    )
    qkv[...] = dot(x[...], weights[...]).astype(jnp.bfloat16)
    row = lax.broadcasted_iota(jnp.int32, (main_rows, main_rows), 0)
    col = lax.broadcasted_iota(jnp.int32, (main_rows, main_rows), 1)
    heads = masked_attention(
        qkv, slice(0, main_rows), (row & 15) == (col & 15)
    ).astype(jnp.bfloat16)
    out[:, : 2 * MAIN, :] = heads.reshape(8, 2 * MAIN, half)
    row = lax.broadcasted_iota(jnp.int32, (tail_rows, tail_rows), 0)
    col = lax.broadcasted_iota(jnp.int32, (tail_rows, tail_rows), 1)
    heads = masked_attention(
        qkv, slice(main_rows, main_rows + tail_rows), ((row ^ col) & 5) == 0
    ).astype(jnp.bfloat16)
    out[:, 2 * MAIN :, :] = heads.reshape(8, 8, half)


def place_kernel(packed, out, tail):
    for d in range(8):
        for f in range(2):
            out[f, MAIN * d : MAIN * d + MAIN, :] = packed[d, MAIN * f : MAIN * f + MAIN, :]
        rest = packed[d, 2 * MAIN :, :].astype(jnp.float32)
        for f in range(2):
            tail[f, 2 * d : 2 * d + 2, :] = rest[2 * f : 2 * f + 2, :]
    for f in range(2):
        out[f, 8 * MAIN :, :] = tail[f].astype(jnp.bfloat16)


def body(
    latents,
    reference_features,
    norm_gain,
    query_weight,
    key_weight,
    value_weight,
    out_weight,
    out_bias,
    motion_gain,
    motion_query,
    motion_key,
    motion_value,
):
    frames, row_count, col_count, channels = latents.shape
    places = row_count * col_count
    width = query_weight.shape[1]
    bf16 = functools.partial(jax.ShapeDtypeStruct, dtype=jnp.bfloat16)
    f32 = functools.partial(jax.ShapeDtypeStruct, dtype=jnp.float32)
    lat = latents.reshape(frames, places, channels)
    gain = norm_gain.reshape(1, channels)
    bias = out_bias.reshape(1, channels)
    motion = motion_gain.reshape(1, channels)

    hbm = pl.BlockSpec(memory_space=pltpu.HBM)
    vmem = pl.BlockSpec(memory_space=pltpu.VMEM)

    def in_hbm(*arrays):
        return tuple(pltpu.with_memory_space_constraint(a, pltpu.HBM) for a in arrays)

    def in_vmem(*arrays):
        return tuple(pltpu.with_memory_space_constraint(a, pltpu.VMEM) for a in arrays)

    def specs(args, held):
        kept = len(args) - held
        return [whole(a) for a in args[:kept]] + [vmem] * held

    def resident(shape):
        return pltpu.VMEM(shape, jnp.bfloat16)

    from_y = send(lat, Y_FLIP)
    from_c = send(lat, C_FLIP)
    own = reference_features
    chip = jnp.concatenate([own, send(own, C_FLIP)], axis=0)
    frame = 2 * (lax.axis_index("tm") % 8)
    codes = lax.dynamic_slice_in_dim(jnp.asarray(position_codes(channels)), frame, 2)
    own_later, chip, codes = lax.optimization_barrier((own, chip, codes))
    from_z = [send(own_later, z_perm(4))] + [send(chip, z_perm(step)) for step in (1, 2, 3)]

    wkv, wq, wo, motion_qkv, flag = call(
        weights_kernel,
        (
            resident((channels, 2 * width)),
            resident((channels, width)),
            resident((width, channels)),
            resident((channels, 3 * width)),
            bf16((16, 128)),
        ),
        in_hbm(
            key_weight,
            value_weight,
            query_weight,
            out_weight,
            motion_query,
            motion_key,
            motion_value,
        ),
        in_specs=[hbm] * 7,
        out_specs=(vmem,) * 4 + (whole(bf16((16, 128))),),
        scratch=[pltpu.SemaphoreType.DMA((7,))],
        moved=11500000,
    )
    tokens = call(
        tokens_kernel,
        bf16((places, channels)),
        (own, *from_z, flag),
        scratch=[pltpu.VMEM((places, channels), jnp.float32)],
        moved=700000,
    )
    from_y, tokens = lax.optimization_barrier((from_y, tokens))
    from_yc = send(from_y, C_FLIP)
    tokens_y = send(tokens, Y_FLIP)
    tokens_c = send(tokens, C_FLIP)

    args = (lat, from_c, from_y, from_yc, gain) + in_vmem(wkv, wq)
    own_parts = call(
        own_kernel,
        (
            bf16((2 * places, width)),
            f32((HEADS, 2 * places, 256)),
            f32((2 * places, 128)),
        ),
        args,
        in_specs=specs(args, 2),
        scratch=[
            pltpu.VMEM((8 * places, channels), jnp.bfloat16),
            pltpu.VMEM((8 * places, channels), jnp.bfloat16),
        ],
        flops=5400000000,
        moved=9000000,
    )
    tokens_y, own_parts = lax.optimization_barrier((tokens_y, own_parts))
    tokens_yc = send(tokens_y, C_FLIP)
    args = (tokens, tokens_c, tokens_y, tokens_yc, *own_parts, lat, bias, motion, codes)
    args += in_vmem(wkv, wo)
    att, packed = call(
        join_kernel,
        (bf16((2 * places, width)), pltpu.HBM((8, 72, width), jnp.bfloat16)),
        args,
        in_specs=specs(args, 2),
        scratch=[
            pltpu.VMEM((4 * places, channels), jnp.bfloat16),
            pltpu.VMEM((4 * places, channels), jnp.bfloat16),
            pltpu.VMEM((2, 16, channels), jnp.float32),
        ],
        flops=2900000000,
        moved=8000000,
    )
    moving = exchange(packed)
    args = (moving,) + in_vmem(motion_qkv)
    rows = 320
    heads = call(
        motion_kernel,
        pltpu.HBM((8, 40, width), jnp.bfloat16),
        args,
        in_specs=specs(args, 1),
        scratch=[
            pltpu.VMEM((rows, channels), jnp.bfloat16),
            pltpu.VMEM((rows, 3 * width), jnp.bfloat16),
        ],
        flops=2200000000,
        moved=8000000,
    )
    returned = exchange(heads)
    args = (lat, att, bias, out_weight, heads)
    block = call(
        block_kernel,
        bf16((2, places, channels)),
        args,
        in_specs=[whole(a) for a in args[:4]] + [hbm],
        flops=500000000,
        moved=3000000,
    )
    motion_heads = call(
        place_kernel,
        bf16((2, places, width)),
        (returned,),
        scratch=[pltpu.VMEM((2, 16, width), jnp.float32)],
        moved=800000,
    )
    return (
        block.reshape(frames, row_count, col_count, channels),
        motion_heads.reshape(frames, row_count, col_count, width),
    )


def solution(mesh):
    return jax.shard_map(
        body,
        mesh=mesh,
        in_specs=(P("tm", "rows", None, None), P(("tm", "rows"), None)) + (P(),) * 10,
        out_specs=(P("tm", "rows", None, None), P("tm", "rows", None, None)),
        check_vma=False,
    )
```

time: 118 us -> 94.9 us (0.80)
  blocking collectives: 0 us -> 27.9 us
  waiting for transfers between devices: 44.6 us -> 20.7 us
  local copies, waits for them, and re-layouts: 14.9 us -> 1.85 us
  starting transfers between devices: 28.8 us -> 17.6 us
  Pallas kernels: 26.6 us -> 24.9 us
    all_to_all x0 -> x1, blocking collectives: none -> 27.9 us  [exchange(): lax.all_to_all(value, 'tm', 0, 0, axis_index_groups=shot_groups(), tiled=...]
    all_to_all x3 -> x1, waiting for transfers between devices: 28.1 us -> 11.5 us  [exchange(): lax.all_to_all(value, 'tm', 0, 0, axis_index_groups=shot_groups(), tiled=...]
    unnamed x36 -> x14, local copies, waits for them, and re-layouts: 12.9 us -> 1.05 us
    all_to_all x3 -> x1, starting transfers between devices: 13.3 us -> 3.46 us  [exchange(): lax.all_to_all(value, 'tm', 0, 0, axis_index_groups=shot_groups(), tiled=...]
    ppermute x13 -> x11, waiting for transfers between devices: 16.5 us -> 9.25 us  [send(): return lax.ppermute(value, AXES, pairs)]
    slice x1 -> x0, local copies, waits for them, and re-layouts: 1.88 us -> none  [body(): from_y = [send(lat[f], Y_FLIP) for f in range(2)]]
    pallas_call x8 -> x7, Pallas kernels: 26.6 us -> 24.9 us  [call(): pl.pallas_call(kernel, out_shape=out_shape, grid=(1,), in_specs=in_specs...]
    ppermute x13 -> x11, starting transfers between devices: 15.5 us -> 14.1 us  [send(): return lax.ppermute(value, AXES, pairs)]
  transfers between devices with their start and end apart: 16 -> 12, of which waited for: 7 -> 7; matrix products, arithmetic and copies ran while one was open for 2% -> 2% of each run, Pallas kernels for 19% -> 15%
where the time goes in v2:
time: 94.9 us; the launch traced here: 94.5 us
  blocking collectives  27.9 us (29%)
  Pallas kernels  24.9 us (26%)
  waiting for transfers between devices  20.7 us (22%)
  starting transfers between devices  17.6 us (19%)
  local copies, waits for them, and re-layouts  1.85 us (2%)
    all_to_all x1, blocking collectives, exchange(): lax.all_to_all(value, 'tm', 0, 0, axis_index_groups=shot_groups(), tiled=...  27.9 us
    pallas_call x7, Pallas kernels, call(): pl.pallas_call(kernel, out_shape=out_shape, grid=(1,), in_specs=in_specs...  24.9 us
    ppermute x11, starting transfers between devices, send(): return lax.ppermute(value, AXES, pairs)  14.1 us
    all_to_all x1, waiting for transfers between devices, exchange(): lax.all_to_all(value, 'tm', 0, 0, axis_index_groups=shot_groups(), tiled=...  11.5 us
    ppermute x11, waiting for transfers between devices, send(): return lax.ppermute(value, AXES, pairs)  9.25 us
    all_to_all x1, starting transfers between devices, exchange(): lax.all_to_all(value, 'tm', 0, 0, axis_index_groups=shot_groups(), tiled=...  3.46 us
  transfers between devices with their start and end apart: 12, of which 7 were waited for; matrix products, arithmetic and copies ran while one was open for 2% of the time, Pallas kernels for 15%

profile of v2, /device:TPU:2, one launch (start us, length us, event | category | flops | bytes accessed | tf_op | source)
XLA Modules:
  0.0 94.5 jit_solution(1322072860420109546)
XLA Ops:
  0.6 3.3 %collective-permute-start = (bf16[2,144,1280]{2,1,0:T(8,128)(2,1)}, bf16[2,144,1280]{2,1,0:T(8,128)(2,1)S(1)}, u32[]{:S(2)}, u32[]{:S(2)}) collective-permute-start(bf16[2,144,1280]{2,1,0:T(8,128)(2,1)} %bitcast.3), channel_id=1, source_target_pairs={{0,2},{1,3},{2,0},{3,1},{4,6},{5,7},{6,4},{7,5},{8,10},{9,11},{10,... | collective-permute-start | bytes 2211848 | tf_op jit(solution)/shard_map/ppermute | solution.py:50
  3.9 0.0 collective-permute-start.1
  3.9 0.8 constant_dynamic-slice_fusion.codes
  4.7 0.7 collective-permute-done.1
  5.4 0.9 pad_maximum_fusion
  6.2 0.0 copy-start.2
  6.2 0.0 copy-start.3
  6.3 0.0 copy-start.4
  6.3 2.0 %collective-permute-start.3 = (bf16[36,1280]{1,0:T(8,128)(2,1)S(1)}, bf16[36,1280]{1,0:T(8,128)(2,1)S(1)}, u32[]{:S(2)}, u32[]{:S(2)}) collective-permute-start(bf16[36,1280]{1,0:T(8,128)(2,1)S(1)} %pad_maximum_fusion), channel_id=1, source_target_pairs={{0,4},{1,29},{2,6},{3,31},{4,8},{5,1},{6,10},{7,3},{8,12},{9,5},{1... | collective-permute-start | bytes 276488 | tf_op jit(solution)/shard_map/ppermute | solution.py:50
  8.3 3.3 %collective-permute-start.4 = (bf16[36,1280]{1,0:T(8,128)(2,1)S(1)}, bf16[36,1280]{1,0:T(8,128)(2,1)S(1)}, u32[]{:S(2)}, u32[]{:S(2)}) collective-permute-start(bf16[36,1280]{1,0:T(8,128)(2,1)S(1)} %pad_maximum_fusion), channel_id=1, source_target_pairs={{0,8},{1,25},{2,10},{3,27},{4,12},{5,29},{6,14},{7,31},{8,16},{9,1... | collective-permute-start | bytes 276488 | tf_op jit(solution)/shard_map/ppermute | solution.py:50
  11.5 4.0 %collective-permute-start.5 = (bf16[36,1280]{1,0:T(8,128)(2,1)S(1)}, bf16[36,1280]{1,0:T(8,128)(2,1)S(1)}, u32[]{:S(2)}, u32[]{:S(2)}) collective-permute-start(bf16[36,1280]{1,0:T(8,128)(2,1)S(1)} %pad_maximum_fusion), channel_id=1, source_target_pairs={{0,12},{1,21},{2,14},{3,23},{4,16},{5,25},{6,18},{7,27},{8,20},{9,... | collective-permute-start | bytes 276488 | tf_op jit(solution)/shard_map/ppermute | solution.py:50
  15.6 0.5 collective-permute-start.2
  16.1 4.4 %shard_map.140 = (bf16[1280,1280]{1,0:T(8,128)(2,1)S(1)}, bf16[1280,640]{1,0:T(8,128)(2,1)S(1)}, bf16[640,1280]{1,0:T(8,128)(2,1)S(1)}, bf16[1280,1920]{1,0:T(8,128)(2,1)S(1)}, bf16[16,128]{1,0:T(8,128)(2,1)S(1)}) custom-call(bf16[1280,640]{1,0:T(8,128)(2,1)} %wk.1, bf16[1280,640]{1,0:T(8,128)(2,1)} %wv.1, bf16[1280,640]{1,0:T(8,128)(2,1)} %wq.1, ...), custom_call_target="tpu_custom_call" | custom-call | bytes 11500000 | tf_op jit(solution)/shard_map/pallas_call | solution.py:73
  20.5 3.6 %collective-permute-done.2.far = bf16[18,1280]{1,0:T(8,128)(2,1)S(1)} collective-permute-done((bf16[18,1280]{1,0:T(8,128)(2,1)}, bf16[18,1280]{1,0:T(8,128)(2,1)S(1)}, u32[]{:S(2)}, u32[]{:S(2)}) %collective-permute-start.2) | collective-permute-done | bytes 46112 | tf_op jit(solution)/shard_map/ppermute | solution.py:50
  24.1 0.0 copy-done.2
  24.1 0.0 collective-permute-start.8
  24.1 0.0 collective-permute-done.3.near1
  24.1 0.0 collective-permute-done.4.near2
  24.1 0.0 collective-permute-done.5.near3
  24.1 0.0 copy-done.3
  24.1 0.1 shard_map.141.t0
  24.2 0.0 collective-permute-done.peer_y
  24.2 0.6 collective-permute-start.9
  24.8 0.0 copy-done.4
  24.8 0.3 collective-permute-start.7
  25.2 0.1 collective-permute-start.6
  25.2 1.1 %collective-permute-done.8.peer_c = bf16[2,144,1280]{2,1,0:T(8,128)(2,1)S(1)} collective-permute-done((bf16[2,144,1280]{2,1,0:T(8,128)(2,1)S(1)}, bf16[2,144,1280]{2,1,0:T(8,128)(2,1)S(1)}, u32[]{:S(2)}, u32[]{:S(2)}) %collective-permute-start.8) | collective-permute-done | bytes 737312 | tf_op jit(solution)/shard_map/ppermute | solution.py:50
  26.3 1.1 %collective-permute-done.9.peer_yc = bf16[2,144,1280]{2,1,0:T(8,128)(2,1)S(1)} collective-permute-done((bf16[2,144,1280]{2,1,0:T(8,128)(2,1)S(1)}, bf16[2,144,1280]{2,1,0:T(8,128)(2,1)S(1)}, u32[]{:S(2)}, u32[]{:S(2)}) %collective-permute-start.9) | collective-permute-done | bytes 737312 | tf_op jit(solution)/shard_map/ppermute | solution.py:50
  27.4 0.0 copy-start.5
  27.4 0.0 copy-start.6
  27.4 8.4 %shard_map.142 = (bf16[288,640]{1,0:T(8,128)(2,1)S(1)}, f32[4,288,256]{2,1,0:T(8,128)S(1)}, f32[288,128]{1,0:T(8,128)S(1)}) custom-call(bf16[2,144,1280]{2,1,0:T(8,128)(2,1)S(1)} %bitcast.5, bf16[2,144,1280]{2,1,0:T(8,128)(2,1)S(1)} %collective-permute-done.8.peer_c, bf16[2,144,1280]{2,1,0:T(8,128)(2,1)S(1)} %collective-permute-done.peer_y, ...), custom_call_target="tpu_custom_call" | custom-call | flops 5400000000 | bytes 9000000 | tf_op jit(solution)/shard_map/pallas_call | solution.py:73
  35.7 1.2 %collective-permute-done.7.t2 = bf16[144,1280]{1,0:T(8,128)(2,1)S(1)} collective-permute-done((bf16[144,1280]{1,0:T(8,128)(2,1)S(1)}, bf16[144,1280]{1,0:T(8,128)(2,1)S(1)}, u32[]{:S(2)}, u32[]{:S(2)}) %collective-permute-start.7) | collective-permute-done | bytes 368672 | tf_op jit(solution)/shard_map/ppermute | solution.py:50
  36.9 0.0 collective-permute-start.10
  36.9 0.0 copy-done.5
  37.0 0.0 copy-done.6
  37.0 0.0 collective-permute-done.6.t1
  37.0 1.6 %collective-permute-done.10.t3 = bf16[144,1280]{1,0:T(8,128)(2,1)S(1)} collective-permute-done((bf16[144,1280]{1,0:T(8,128)(2,1)S(1)}, bf16[144,1280]{1,0:T(8,128)(2,1)S(1)}, u32[]{:S(2)}, u32[]{:S(2)}) %collective-permute-start.10) | collective-permute-done | bytes 368672 | tf_op jit(solution)/shard_map/ppermute | solution.py:50
  38.6 6.4 %shard_map.143 = (bf16[288,640]{1,0:T(8,128)(2,1)S(1)}, bf16[8,72,640]{2,1,0:T(8,128)(2,1)}) custom-call(bf16[144,1280]{1,0:T(8,128)(2,1)S(1)} %shard_map.141.t0, bf16[144,1280]{1,0:T(8,128)(2,1)S(1)} %collective-permute-done.6.t1, bf16[144,1280]{1,0:T(8,128)(2,1)S(1)} %collective-permute-done.7.t2, bf16[144,1280]{1,0:T(8,128)(2,1)S(1)} %collective-permute-done.10.t3, ...), custom_call_target="tpu_custom_call" | custom-call | flops 2900000000 | bytes 8000000 | tf_op jit(solution)/shard_map/pallas_call | solution.py:73
  45.0 27.9 %all_to_all.10.moving = bf16[8,72,640]{2,1,0:T(8,128)(2,1)S(1)} all-to-all(bf16[8,72,640]{2,1,0:T(8,128)(2,1)} %get-tuple-element.38), channel_id=1, replica_groups={{0,4,8,12,16,20,24,28},{32,36,40,44,48,52,56,60},{64,68,72,76,80,84,88,..., dimensions={0} | all-to-all | bytes 1474560 | tf_op jit(solution)/shard_map/all_to_all | solution.py:58
  72.9 0.0 copy-start
  72.9 3.2 %shard_map.144.after = bf16[8,40,640]{2,1,0:T(8,128)(2,1)} custom-call(bf16[8,72,640]{2,1,0:T(8,128)(2,1)S(1)} %all_to_all.10.moving, bf16[1280,1920]{1,0:T(8,128)(2,1)S(1)} %get-tuple-element.39.weights), custom_call_target="tpu_custom_call" | custom-call | flops 2200000000 | bytes 8000000 | tf_op jit(solution)/shard_map/pallas_call | solution.py:73
  76.1 3.5 %all-to-all-start.1 = ((bf16[8,40,640]{2,1,0:T(8,128)(2,1)}), bf16[8,40,640]{2,1,0:T(8,128)(2,1)S(1)}, u32[]{:S(2)}, u32[]{:S(2)}) async-start(bf16[8,40,640]{2,1,0:T(8,128)(2,1)} %shard_map.144.after), calls=%async_computation.1 | async-start | bytes 819200 | tf_op jit(solution)/shard_map/all_to_all | solution.py:58
  79.6 0.0 copy-done
  79.6 0.0 copy-start.1
  79.6 1.0 %copy-done.1 = bf16[8,40,640]{2,1,0:T(8,128)(2,1)S(1)} copy-done((bf16[8,40,640]{2,1,0:T(8,128)(2,1)S(1)}, bf16[8,40,640]{2,1,0:T(8,128)(2,1)}, u32[]{:S(2)}) %copy-start.1) | copy-done | bytes 409624
  80.7 1.6 %shard_map.145 = bf16[2,144,1280]{2,1,0:T(8,128)(2,1)} custom-call(bf16[2,144,1280]{2,1,0:T(8,128)(2,1)S(1)} %bitcast.7, bf16[288,640]{1,0:T(8,128)(2,1)S(1)} %get-tuple-element.37.att, f32[1,1280]{1,0:T(1,128)S(1)} %reshape.24.bias, bf16[640,1280]{1,0:T(8,128)(2,1)S(1)} %copy-done, bf16[8,40,640]{2,1,0:T(8,128)(2,1)S(1)} %copy-done.1), custom_call_target="tpu_custom_call" | custom-call | flops 500000000 | bytes 3000000 | tf_op jit(solution)/shard_map/pallas_call | solution.py:73
  82.3 11.5 %all-to-all-done.1.packed = bf16[8,40,640]{2,1,0:T(8,128)(2,1)S(1)} async-done(((bf16[8,40,640]{2,1,0:T(8,128)(2,1)}), bf16[8,40,640]{2,1,0:T(8,128)(2,1)S(1)}, u32[]{:S(2)}, u32[]{:S(2)}) %all-to-all-start.1) | async-done | bytes 409632 | tf_op jit(solution)/shard_map/all_to_all | solution.py:58
  93.7 0.8 shard_map.146
  (3 shorter events, 0.0 us)
Async XLA Ops:
  0.6 23.6 %collective-permute-start = (bf16[2,144,1280]{2,1,0:T(8,128)(2,1)}, bf16[2,144,1280]{2,1,0:T(8,128)(2,1)S(1)}, u32[]{:S(2)}, u32[]{:S(2)}) collective-permute-start(bf16[2,144,1280]{2,1,0:T(8,128)(2,1)} %bitcast.3), channel_id=1, source_target_pairs={{0,2},{1,3},{2,0},{3,1},{4,6},{5,7},{6,4},{7,5},{8,10},{9,11},{10,... | collective-permute-start | bytes 2211848 | tf_op jit(solution)/shard_map/ppermute | solution.py:50
  3.9 1.5 %collective-permute-start.1 = (bf16[18,1280]{1,0:T(8,128)(2,1)}, bf16[18,1280]{1,0:T(8,128)(2,1)S(1)}, u32[]{:S(2)}, u32[]{:S(2)}) collective-permute-start(bf16[18,1280]{1,0:T(8,128)(2,1)} %own.1), channel_id=1, source_target_pairs={{0,1},{1,0},{2,3},{3,2},{4,5},{5,4},{6,7},{7,6},{8,9},{9,8},{10,11... | collective-permute-start | bytes 138248 | tf_op jit(solution)/shard_map/ppermute | solution.py:50
  6.2 17.9 %copy-start.2 = (bf16[2,6,24,1280]{3,2,1,0:T(8,128)(2,1)S(1)}, bf16[2,6,24,1280]{3,2,1,0:T(8,128)(2,1)}, u32[]{:S(2)}) copy-start(bf16[2,6,24,1280]{3,2,1,0:T(8,128)(2,1)} %param.13) | copy-start | bytes 2211844
  6.2 17.9 %copy-start.3 = (bf16[18,1280]{1,0:T(8,128)(2,1)S(1)}, bf16[18,1280]{1,0:T(8,128)(2,1)}, u32[]{:S(2)}) copy-start(bf16[18,1280]{1,0:T(8,128)(2,1)} %own.1) | copy-start | bytes 138244
  6.3 18.6 %copy-start.4 = (f32[1280]{0:T(1024)S(1)}, f32[1280]{0:T(1024)}, u32[]{:S(2)}) copy-start(f32[1280]{0:T(1024)} %param.15) | copy-start | bytes 15364
  6.3 17.8 %collective-permute-start.3 = (bf16[36,1280]{1,0:T(8,128)(2,1)S(1)}, bf16[36,1280]{1,0:T(8,128)(2,1)S(1)}, u32[]{:S(2)}, u32[]{:S(2)}) collective-permute-start(bf16[36,1280]{1,0:T(8,128)(2,1)S(1)} %pad_maximum_fusion), channel_id=1, source_target_pairs={{0,4},{1,29},{2,6},{3,31},{4,8},{5,1},{6,10},{7,3},{8,12},{9,5},{1... | collective-permute-start | bytes 276488 | tf_op jit(solution)/shard_map/ppermute | solution.py:50
  8.3 15.9 %collective-permute-start.4 = (bf16[36,1280]{1,0:T(8,128)(2,1)S(1)}, bf16[36,1280]{1,0:T(8,128)(2,1)S(1)}, u32[]{:S(2)}, u32[]{:S(2)}) collective-permute-start(bf16[36,1280]{1,0:T(8,128)(2,1)S(1)} %pad_maximum_fusion), channel_id=1, source_target_pairs={{0,8},{1,25},{2,10},{3,27},{4,12},{5,29},{6,14},{7,31},{8,16},{9,1... | collective-permute-start | bytes 276488 | tf_op jit(solution)/shard_map/ppermute | solution.py:50
  11.5 12.6 %collective-permute-start.5 = (bf16[36,1280]{1,0:T(8,128)(2,1)S(1)}, bf16[36,1280]{1,0:T(8,128)(2,1)S(1)}, u32[]{:S(2)}, u32[]{:S(2)}) collective-permute-start(bf16[36,1280]{1,0:T(8,128)(2,1)S(1)} %pad_maximum_fusion), channel_id=1, source_target_pairs={{0,12},{1,21},{2,14},{3,23},{4,16},{5,25},{6,18},{7,27},{8,20},{9,... | collective-permute-start | bytes 276488 | tf_op jit(solution)/shard_map/ppermute | solution.py:50
  15.6 8.5 %collective-permute-start.2 = (bf16[18,1280]{1,0:T(8,128)(2,1)}, bf16[18,1280]{1,0:T(8,128)(2,1)S(1)}, u32[]{:S(2)}, u32[]{:S(2)}) collective-permute-start(bf16[18,1280]{1,0:T(8,128)(2,1)} %own.1), channel_id=1, source_target_pairs={{0,16},{1,17},{2,18},{3,19},{4,20},{5,21},{6,22},{7,23},{8,24},{9,... | collective-permute-start | bytes 138248 | tf_op jit(solution)/shard_map/ppermute | solution.py:50
  24.1 2.2 %collective-permute-start.8 = (bf16[2,144,1280]{2,1,0:T(8,128)(2,1)S(1)}, bf16[2,144,1280]{2,1,0:T(8,128)(2,1)S(1)}, u32[]{:S(2)}, u32[]{:S(2)}) collective-permute-start(bf16[2,144,1280]{2,1,0:T(8,128)(2,1)S(1)} %bitcast.4), channel_id=1, source_target_pairs={{0,1},{1,0},{2,3},{3,2},{4,5},{5,4},{6,7},{7,6},{8,9},{9,8},{10,11... | collective-permute-start | bytes 2211848 | tf_op jit(solution)/shard_map/ppermute | solution.py:50
  24.2 3.1 %collective-permute-start.9 = (bf16[2,144,1280]{2,1,0:T(8,128)(2,1)S(1)}, bf16[2,144,1280]{2,1,0:T(8,128)(2,1)S(1)}, u32[]{:S(2)}, u32[]{:S(2)}) collective-permute-start(bf16[2,144,1280]{2,1,0:T(8,128)(2,1)S(1)} %collective-permute-done.peer_y), channel_id=1, source_target_pairs={{0,1},{1,0},{2,3},{3,2},{4,5},{5,4},{6,7},{7,6},{8,9},{9,8},{10,11... | collective-permute-start | bytes 2211848 | tf_op jit(solution)/shard_map/ppermute | solution.py:50
  24.8 12.1 %collective-permute-start.7 = (bf16[144,1280]{1,0:T(8,128)(2,1)S(1)}, bf16[144,1280]{1,0:T(8,128)(2,1)S(1)}, u32[]{:S(2)}, u32[]{:S(2)}) collective-permute-start(bf16[144,1280]{1,0:T(8,128)(2,1)S(1)} %shard_map.141.t0), channel_id=1, source_target_pairs={{0,2},{1,3},{2,0},{3,1},{4,6},{5,7},{6,4},{7,5},{8,10},{9,11},{10,... | collective-permute-start | bytes 1105928 | tf_op jit(solution)/shard_map/ppermute | solution.py:50
  25.2 11.8 %collective-permute-start.6 = (bf16[144,1280]{1,0:T(8,128)(2,1)S(1)}, bf16[144,1280]{1,0:T(8,128)(2,1)S(1)}, u32[]{:S(2)}, u32[]{:S(2)}) collective-permute-start(bf16[144,1280]{1,0:T(8,128)(2,1)S(1)} %shard_map.141.t0), channel_id=1, source_target_pairs={{0,1},{1,0},{2,3},{3,2},{4,5},{5,4},{6,7},{7,6},{8,9},{9,8},{10,11... | collective-permute-start | bytes 1105928 | tf_op jit(solution)/shard_map/ppermute | solution.py:50
  27.4 9.6 %copy-start.5 = (f32[1280]{0:T(1024)S(1)}, f32[1280]{0:T(1024)}, u32[]{:S(2)}) copy-start(f32[1280]{0:T(1024)} %param.20) | copy-start | bytes 15364
  27.4 9.6 %copy-start.6 = (f32[1280]{0:T(1024)S(1)}, f32[1280]{0:T(1024)}, u32[]{:S(2)}) copy-start(f32[1280]{0:T(1024)} %param.21) | copy-start | bytes 15364
  36.9 1.7 %collective-permute-start.10 = (bf16[144,1280]{1,0:T(8,128)(2,1)S(1)}, bf16[144,1280]{1,0:T(8,128)(2,1)S(1)}, u32[]{:S(2)}, u32[]{:S(2)}) collective-permute-start(bf16[144,1280]{1,0:T(8,128)(2,1)S(1)} %collective-permute-done.7.t2), channel_id=1, source_target_pairs={{0,1},{1,0},{2,3},{3,2},{4,5},{5,4},{6,7},{7,6},{8,9},{9,8},{10,11... | collective-permute-start | bytes 1105928 | tf_op jit(solution)/shard_map/ppermute | solution.py:50
  72.9 6.7 %copy-start = (bf16[640,1280]{1,0:T(8,128)(2,1)S(1)}, bf16[640,1280]{1,0:T(8,128)(2,1)}, u32[]{:S(2)}) copy-start(bf16[640,1280]{1,0:T(8,128)(2,1)} %wo.3) | copy-start | bytes 4915204
  76.1 17.6 %all-to-all-start.1 = ((bf16[8,40,640]{2,1,0:T(8,128)(2,1)}), bf16[8,40,640]{2,1,0:T(8,128)(2,1)S(1)}, u32[]{:S(2)}, u32[]{:S(2)}) async-start(bf16[8,40,640]{2,1,0:T(8,128)(2,1)} %shard_map.144.after), calls=%async_computation.1 | async-start | bytes 819200 | tf_op jit(solution)/shard_map/all_to_all | solution.py:58
  79.6 1.0 %copy-start.1 = (bf16[8,40,640]{2,1,0:T(8,128)(2,1)S(1)}, bf16[8,40,640]{2,1,0:T(8,128)(2,1)}, u32[]{:S(2)}) copy-start(bf16[8,40,640]{2,1,0:T(8,128)(2,1)} %shard_map.144.after) | copy-start | bytes 1228804

commit v3 on v2

--- a/solution.py
+++ b/solution.py
@@ -190,7 +190,7 @@
 
 
 def join_kernel(
-    t0, t1, t2, t3, q, o, ml, lat, bias, gain, codes, wkv, wo, att_out, packed, tokens, kv, tail
+    t0, t1, t2, t3, q, o, ml, lat, bias, gain, codes, wkv, wo, block_out, packed, tokens, kv, tail
 ):
     places, channels = t0.shape
     width = channels // 2
@@ -210,11 +210,13 @@
         total = ml[:, HEADS + h : HEADS + h + 1] * keep + jnp.sum(p, axis=1, keepdims=True)
         mixed = o[h] * keep + dot(p.astype(jnp.bfloat16), kv[:, width + w : width + w + 256])
         parts.append(mixed * (1.0 / total))
-    att_out[...] = side_by_side(parts).astype(jnp.bfloat16)
+    att = side_by_side(parts).astype(jnp.bfloat16)
     for f in range(2):
         mine = slice(f * places, (f + 1) * places)
-        block = lat[f].astype(jnp.float32) + dot(att_out[mine, :], wo[...]) + bias[...]
-        block = block.astype(jnp.bfloat16).astype(jnp.float32)
+        block = lat[f].astype(jnp.float32) + dot(att[mine, :], wo[...]) + bias[...]
+        block = block.astype(jnp.bfloat16)
+        block_out[f] = block
+        block = block.astype(jnp.float32)
         moving = layer_norm(block, gain[...], codes[f : f + 1, :])
         tail[f] = moving[8 * MAIN :, :]
         moving = moving.astype(jnp.bfloat16)
@@ -260,15 +262,6 @@
     flag[...] = jnp.zeros_like(flag)
     for copy in copies:
         copy.wait()
-
-
-def block_kernel(lat, att, bias, wo, after, out):
-    places = lat.shape[1]
-    for f in range(2):
-        mine = slice(f * places, (f + 1) * places)
-        out[f] = (
-            lat[f].astype(jnp.float32) + dot(att[mine, :], wo[...]) + bias[...]
-        ).astype(jnp.bfloat16)
 
 
 def layer_norm(x, gain, codes):
@@ -441,9 +434,9 @@
     tokens_yc = send(tokens_y, C_FLIP)
     args = (tokens, tokens_c, tokens_y, tokens_yc, *own_parts, lat, bias, motion, codes)
     args += in_vmem(wkv, wo)
-    att, packed = call(
+    block, packed = call(
         join_kernel,
-        (bf16((2 * places, width)), pltpu.HBM((8, 72, width), jnp.bfloat16)),
+        (bf16((2, places, channels)), bf16((8, 72, width))),
         args,
         in_specs=specs(args, 2),
         scratch=[
@@ -459,7 +452,7 @@
     rows = 320
     heads = call(
         motion_kernel,
-        pltpu.HBM((8, 40, width), jnp.bfloat16),
+        bf16((8, 40, width)),
         args,
         in_specs=specs(args, 1),
         scratch=[
@@ -470,15 +463,6 @@
         moved=8000000,
     )
     returned = exchange(heads)
-    args = (lat, att, bias, out_weight, heads)
-    block = call(
-        block_kernel,
-        bf16((2, places, channels)),
-        args,
-        in_specs=[whole(a) for a in args[:4]] + [hbm],
-        flops=500000000,
-        moved=3000000,
-    )
     motion_heads = call(
         place_kernel,
         bf16((2, places, width)),

time: 94.9 us -> 92.5 us (0.975)
  blocking collectives: 27.9 us -> 44.3 us
  waiting for transfers between devices: 20.7 us -> 9.25 us
  starting transfers between devices: 17.6 us -> 14.1 us
  Pallas kernels: 24.9 us -> 22.2 us
  local copies, waits for them, and re-layouts: 1.85 us -> 0.83 us
    all_to_all x1 -> x2, blocking collectives: 27.9 us -> 44.3 us  [exchange(): lax.all_to_all(value, 'tm', 0, 0, axis_index_groups=shot_groups(), tiled=...]
    all_to_all x1 -> x0, waiting for transfers between devices: 11.5 us -> none  [exchange(): lax.all_to_all(value, 'tm', 0, 0, axis_index_groups=shot_groups(), tiled=...]
    all_to_all x1 -> x0, starting transfers between devices: 3.46 us -> none  [exchange(): lax.all_to_all(value, 'tm', 0, 0, axis_index_groups=shot_groups(), tiled=...]
    pallas_call x7 -> x6, Pallas kernels: 24.9 us -> 22.2 us  [call(): pl.pallas_call(kernel, out_shape=out_shape, grid=(1,), in_specs=in_specs...]
    unnamed x14 -> x10, local copies, waits for them, and re-layouts: 1.05 us -> 0.03 us
  transfers between devices with their start and end apart: 12 -> 11, of which waited for: 7 -> 6; matrix products, arithmetic and copies ran while one was open for 2% -> 2% of each run, Pallas kernels for 15% -> 14%
where the time goes in v3:
time: 92.5 us; the launch traced here: 92.3 us
  blocking collectives  44.3 us (48%)
  Pallas kernels  22.2 us (24%)
  starting transfers between devices  14.1 us (15%)
  waiting for transfers between devices  9.25 us (10%)
    all_to_all x2, blocking collectives, exchange(): lax.all_to_all(value, 'tm', 0, 0, axis_index_groups=shot_groups(), tiled=...  44.3 us
    pallas_call x6, Pallas kernels, call(): pl.pallas_call(kernel, out_shape=out_shape, grid=(1,), in_specs=in_specs...  22.2 us
    ppermute x11, starting transfers between devices, send(): return lax.ppermute(value, AXES, pairs)  14.1 us
    ppermute x11, waiting for transfers between devices, send(): return lax.ppermute(value, AXES, pairs)  9.25 us
  transfers between devices with their start and end apart: 11, of which 6 were waited for; matrix products, arithmetic and copies ran while one was open for 2% of the time, Pallas kernels for 14%

profile of v3, /device:TPU:2, one launch (start us, length us, event | category | flops | bytes accessed | tf_op | source)
XLA Modules:
  0.0 92.3 jit_solution(17282452089991820657)
XLA Ops:
  0.6 3.3 %collective-permute-start = (bf16[2,144,1280]{2,1,0:T(8,128)(2,1)}, bf16[2,144,1280]{2,1,0:T(8,128)(2,1)S(1)}, u32[]{:S(2)}, u32[]{:S(2)}) collective-permute-start(bf16[2,144,1280]{2,1,0:T(8,128)(2,1)} %bitcast.3), channel_id=1, source_target_pairs={{0,2},{1,3},{2,0},{3,1},{4,6},{5,7},{6,4},{7,5},{8,10},{9,11},{10,... | collective-permute-start | bytes 2211848 | tf_op jit(solution)/shard_map/ppermute | solution.py:50
  3.9 0.0 collective-permute-start.1
  3.9 0.8 constant_dynamic-slice_fusion.codes
  4.7 0.7 collective-permute-done.1
  5.4 0.9 pad_maximum_fusion
  6.2 0.0 copy-start.1
  6.2 0.0 copy-start
  6.2 0.0 copy-start.2
  6.3 2.0 %collective-permute-start.3 = (bf16[36,1280]{1,0:T(8,128)(2,1)S(1)}, bf16[36,1280]{1,0:T(8,128)(2,1)S(1)}, u32[]{:S(2)}, u32[]{:S(2)}) collective-permute-start(bf16[36,1280]{1,0:T(8,128)(2,1)S(1)} %pad_maximum_fusion), channel_id=1, source_target_pairs={{0,4},{1,29},{2,6},{3,31},{4,8},{5,1},{6,10},{7,3},{8,12},{9,5},{1... | collective-permute-start | bytes 276488 | tf_op jit(solution)/shard_map/ppermute | solution.py:50
  8.3 3.3 %collective-permute-start.4 = (bf16[36,1280]{1,0:T(8,128)(2,1)S(1)}, bf16[36,1280]{1,0:T(8,128)(2,1)S(1)}, u32[]{:S(2)}, u32[]{:S(2)}) collective-permute-start(bf16[36,1280]{1,0:T(8,128)(2,1)S(1)} %pad_maximum_fusion), channel_id=1, source_target_pairs={{0,8},{1,25},{2,10},{3,27},{4,12},{5,29},{6,14},{7,31},{8,16},{9,1... | collective-permute-start | bytes 276488 | tf_op jit(solution)/shard_map/ppermute | solution.py:50
  11.5 4.0 %collective-permute-start.5 = (bf16[36,1280]{1,0:T(8,128)(2,1)S(1)}, bf16[36,1280]{1,0:T(8,128)(2,1)S(1)}, u32[]{:S(2)}, u32[]{:S(2)}) collective-permute-start(bf16[36,1280]{1,0:T(8,128)(2,1)S(1)} %pad_maximum_fusion), channel_id=1, source_target_pairs={{0,12},{1,21},{2,14},{3,23},{4,16},{5,25},{6,18},{7,27},{8,20},{9,... | collective-permute-start | bytes 276488 | tf_op jit(solution)/shard_map/ppermute | solution.py:50
  15.6 0.5 collective-permute-start.2
  16.1 4.4 %shard_map.140 = (bf16[1280,1280]{1,0:T(8,128)(2,1)S(1)}, bf16[1280,640]{1,0:T(8,128)(2,1)S(1)}, bf16[640,1280]{1,0:T(8,128)(2,1)S(1)}, bf16[1280,1920]{1,0:T(8,128)(2,1)S(1)}, bf16[16,128]{1,0:T(8,128)(2,1)S(1)}) custom-call(bf16[1280,640]{1,0:T(8,128)(2,1)} %wk.1, bf16[1280,640]{1,0:T(8,128)(2,1)} %wv.1, bf16[1280,640]{1,0:T(8,128)(2,1)} %wq.1, ...), custom_call_target="tpu_custom_call" | custom-call | bytes 11500000 | tf_op jit(solution)/shard_map/pallas_call | solution.py:73
  20.5 3.6 %collective-permute-done.2.far = bf16[18,1280]{1,0:T(8,128)(2,1)S(1)} collective-permute-done((bf16[18,1280]{1,0:T(8,128)(2,1)}, bf16[18,1280]{1,0:T(8,128)(2,1)S(1)}, u32[]{:S(2)}, u32[]{:S(2)}) %collective-permute-start.2) | collective-permute-done | bytes 46112 | tf_op jit(solution)/shard_map/ppermute | solution.py:50
  24.1 0.0 copy-done.1
  24.1 0.0 collective-permute-start.8
  24.1 0.0 collective-permute-done.3.near1
  24.1 0.0 collective-permute-done.4.near2
  24.1 0.0 collective-permute-done.5.near3
  24.1 0.0 copy-done
  24.1 0.1 shard_map.141.t0
  24.2 0.0 collective-permute-done.peer_y
  24.2 0.6 collective-permute-start.9
  24.8 0.0 copy-done.2
  24.8 0.3 collective-permute-start.7
  25.2 0.1 collective-permute-start.6
  25.2 1.1 %collective-permute-done.8.peer_c = bf16[2,144,1280]{2,1,0:T(8,128)(2,1)S(1)} collective-permute-done((bf16[2,144,1280]{2,1,0:T(8,128)(2,1)S(1)}, bf16[2,144,1280]{2,1,0:T(8,128)(2,1)S(1)}, u32[]{:S(2)}, u32[]{:S(2)}) %collective-permute-start.8) | collective-permute-done | bytes 737312 | tf_op jit(solution)/shard_map/ppermute | solution.py:50
  26.3 1.1 %collective-permute-done.9.peer_yc = bf16[2,144,1280]{2,1,0:T(8,128)(2,1)S(1)} collective-permute-done((bf16[2,144,1280]{2,1,0:T(8,128)(2,1)S(1)}, bf16[2,144,1280]{2,1,0:T(8,128)(2,1)S(1)}, u32[]{:S(2)}, u32[]{:S(2)}) %collective-permute-start.9) | collective-permute-done | bytes 737312 | tf_op jit(solution)/shard_map/ppermute | solution.py:50
  27.4 0.0 copy-start.3
  27.4 0.0 copy-start.4
  27.4 8.4 %shard_map.142 = (bf16[288,640]{1,0:T(8,128)(2,1)S(1)}, f32[4,288,256]{2,1,0:T(8,128)S(1)}, f32[288,128]{1,0:T(8,128)S(1)}) custom-call(bf16[2,144,1280]{2,1,0:T(8,128)(2,1)S(1)} %bitcast.5, bf16[2,144,1280]{2,1,0:T(8,128)(2,1)S(1)} %collective-permute-done.8.peer_c, bf16[2,144,1280]{2,1,0:T(8,128)(2,1)S(1)} %collective-permute-done.peer_y, ...), custom_call_target="tpu_custom_call" | custom-call | flops 5400000000 | bytes 9000000 | tf_op jit(solution)/shard_map/pallas_call | solution.py:73
  35.7 1.2 %collective-permute-done.7.t2 = bf16[144,1280]{1,0:T(8,128)(2,1)S(1)} collective-permute-done((bf16[144,1280]{1,0:T(8,128)(2,1)S(1)}, bf16[144,1280]{1,0:T(8,128)(2,1)S(1)}, u32[]{:S(2)}, u32[]{:S(2)}) %collective-permute-start.7) | collective-permute-done | bytes 368672 | tf_op jit(solution)/shard_map/ppermute | solution.py:50
  36.9 0.0 collective-permute-start.10
  36.9 0.0 copy-done.3
  37.0 0.0 copy-done.4
  37.0 0.0 collective-permute-done.6.t1
  37.0 1.6 %collective-permute-done.10.t3 = bf16[144,1280]{1,0:T(8,128)(2,1)S(1)} collective-permute-done((bf16[144,1280]{1,0:T(8,128)(2,1)S(1)}, bf16[144,1280]{1,0:T(8,128)(2,1)S(1)}, u32[]{:S(2)}, u32[]{:S(2)}) %collective-permute-start.10) | collective-permute-done | bytes 368672 | tf_op jit(solution)/shard_map/ppermute | solution.py:50
  38.6 6.1 %shard_map.143 = (bf16[2,144,1280]{2,1,0:T(8,128)(2,1)}, bf16[8,72,640]{2,1,0:T(8,128)(2,1)S(1)}) custom-call(bf16[144,1280]{1,0:T(8,128)(2,1)S(1)} %shard_map.141.t0, bf16[144,1280]{1,0:T(8,128)(2,1)S(1)} %collective-permute-done.6.t1, bf16[144,1280]{1,0:T(8,128)(2,1)S(1)} %collective-permute-done.7.t2, bf16[144,1280]{1,0:T(8,128)(2,1)S(1)} %collective-permute-done.10.t3, ...), custom_call_target="tpu_custom_call" | custom-call | flops 2900000000 | bytes 8000000 | tf_op jit(solution)/shard_map/pallas_call | solution.py:73
  44.7 27.7 %all_to_all.10.moving = bf16[8,72,640]{2,1,0:T(8,128)(2,1)S(1)} all-to-all(bf16[8,72,640]{2,1,0:T(8,128)(2,1)S(1)} %get-tuple-element.38), channel_id=1, replica_groups={{0,4,8,12,16,20,24,28},{32,36,40,44,48,52,56,60},{64,68,72,76,80,84,88,..., dimensions={0} | all-to-all | bytes 1474560 | tf_op jit(solution)/shard_map/all_to_all | solution.py:58
  72.4 2.5 %shard_map.144 = bf16[8,40,640]{2,1,0:T(8,128)(2,1)S(1)} custom-call(bf16[8,72,640]{2,1,0:T(8,128)(2,1)S(1)} %all_to_all.10.moving, bf16[1280,1920]{1,0:T(8,128)(2,1)S(1)} %get-tuple-element.39.weights), custom_call_target="tpu_custom_call" | custom-call | flops 2200000000 | bytes 8000000 | tf_op jit(solution)/shard_map/pallas_call | solution.py:73
  74.9 16.6 %all_to_all.11.packed = bf16[8,40,640]{2,1,0:T(8,128)(2,1)S(1)} all-to-all(bf16[8,40,640]{2,1,0:T(8,128)(2,1)S(1)} %shard_map.144), channel_id=1, replica_groups={{0,4,8,12,16,20,24,28},{32,36,40,44,48,52,56,60},{64,68,72,76,80,84,88,..., dimensions={0} | all-to-all | bytes 819200 | tf_op jit(solution)/shard_map/all_to_all | solution.py:58
  91.5 0.8 shard_map.145
  (3 shorter events, 0.0 us)
Async XLA Ops:
  0.6 23.6 %collective-permute-start = (bf16[2,144,1280]{2,1,0:T(8,128)(2,1)}, bf16[2,144,1280]{2,1,0:T(8,128)(2,1)S(1)}, u32[]{:S(2)}, u32[]{:S(2)}) collective-permute-start(bf16[2,144,1280]{2,1,0:T(8,128)(2,1)} %bitcast.3), channel_id=1, source_target_pairs={{0,2},{1,3},{2,0},{3,1},{4,6},{5,7},{6,4},{7,5},{8,10},{9,11},{10,... | collective-permute-start | bytes 2211848 | tf_op jit(solution)/shard_map/ppermute | solution.py:50
  3.9 1.5 %collective-permute-start.1 = (bf16[18,1280]{1,0:T(8,128)(2,1)}, bf16[18,1280]{1,0:T(8,128)(2,1)S(1)}, u32[]{:S(2)}, u32[]{:S(2)}) collective-permute-start(bf16[18,1280]{1,0:T(8,128)(2,1)} %own.1), channel_id=1, source_target_pairs={{0,1},{1,0},{2,3},{3,2},{4,5},{5,4},{6,7},{7,6},{8,9},{9,8},{10,11... | collective-permute-start | bytes 138248 | tf_op jit(solution)/shard_map/ppermute | solution.py:50
  6.2 17.9 %copy-start.1 = (bf16[2,6,24,1280]{3,2,1,0:T(8,128)(2,1)S(1)}, bf16[2,6,24,1280]{3,2,1,0:T(8,128)(2,1)}, u32[]{:S(2)}) copy-start(bf16[2,6,24,1280]{3,2,1,0:T(8,128)(2,1)} %param.13) | copy-start | bytes 2211844
  6.2 17.9 %copy-start = (bf16[18,1280]{1,0:T(8,128)(2,1)S(1)}, bf16[18,1280]{1,0:T(8,128)(2,1)}, u32[]{:S(2)}) copy-start(bf16[18,1280]{1,0:T(8,128)(2,1)} %own.1) | copy-start | bytes 138244
  6.2 18.6 %copy-start.2 = (f32[1280]{0:T(1024)S(1)}, f32[1280]{0:T(1024)}, u32[]{:S(2)}) copy-start(f32[1280]{0:T(1024)} %param.15) | copy-start | bytes 15364
  6.3 17.8 %collective-permute-start.3 = (bf16[36,1280]{1,0:T(8,128)(2,1)S(1)}, bf16[36,1280]{1,0:T(8,128)(2,1)S(1)}, u32[]{:S(2)}, u32[]{:S(2)}) collective-permute-start(bf16[36,1280]{1,0:T(8,128)(2,1)S(1)} %pad_maximum_fusion), channel_id=1, source_target_pairs={{0,4},{1,29},{2,6},{3,31},{4,8},{5,1},{6,10},{7,3},{8,12},{9,5},{1... | collective-permute-start | bytes 276488 | tf_op jit(solution)/shard_map/ppermute | solution.py:50
  8.3 15.9 %collective-permute-start.4 = (bf16[36,1280]{1,0:T(8,128)(2,1)S(1)}, bf16[36,1280]{1,0:T(8,128)(2,1)S(1)}, u32[]{:S(2)}, u32[]{:S(2)}) collective-permute-start(bf16[36,1280]{1,0:T(8,128)(2,1)S(1)} %pad_maximum_fusion), channel_id=1, source_target_pairs={{0,8},{1,25},{2,10},{3,27},{4,12},{5,29},{6,14},{7,31},{8,16},{9,1... | collective-permute-start | bytes 276488 | tf_op jit(solution)/shard_map/ppermute | solution.py:50
  11.5 12.6 %collective-permute-start.5 = (bf16[36,1280]{1,0:T(8,128)(2,1)S(1)}, bf16[36,1280]{1,0:T(8,128)(2,1)S(1)}, u32[]{:S(2)}, u32[]{:S(2)}) collective-permute-start(bf16[36,1280]{1,0:T(8,128)(2,1)S(1)} %pad_maximum_fusion), channel_id=1, source_target_pairs={{0,12},{1,21},{2,14},{3,23},{4,16},{5,25},{6,18},{7,27},{8,20},{9,... | collective-permute-start | bytes 276488 | tf_op jit(solution)/shard_map/ppermute | solution.py:50
  15.6 8.5 %collective-permute-start.2 = (bf16[18,1280]{1,0:T(8,128)(2,1)}, bf16[18,1280]{1,0:T(8,128)(2,1)S(1)}, u32[]{:S(2)}, u32[]{:S(2)}) collective-permute-start(bf16[18,1280]{1,0:T(8,128)(2,1)} %own.1), channel_id=1, source_target_pairs={{0,16},{1,17},{2,18},{3,19},{4,20},{5,21},{6,22},{7,23},{8,24},{9,... | collective-permute-start | bytes 138248 | tf_op jit(solution)/shard_map/ppermute | solution.py:50
  24.1 2.2 %collective-permute-start.8 = (bf16[2,144,1280]{2,1,0:T(8,128)(2,1)S(1)}, bf16[2,144,1280]{2,1,0:T(8,128)(2,1)S(1)}, u32[]{:S(2)}, u32[]{:S(2)}) collective-permute-start(bf16[2,144,1280]{2,1,0:T(8,128)(2,1)S(1)} %bitcast.4), channel_id=1, source_target_pairs={{0,1},{1,0},{2,3},{3,2},{4,5},{5,4},{6,7},{7,6},{8,9},{9,8},{10,11... | collective-permute-start | bytes 2211848 | tf_op jit(solution)/shard_map/ppermute | solution.py:50
  24.2 3.1 %collective-permute-start.9 = (bf16[2,144,1280]{2,1,0:T(8,128)(2,1)S(1)}, bf16[2,144,1280]{2,1,0:T(8,128)(2,1)S(1)}, u32[]{:S(2)}, u32[]{:S(2)}) collective-permute-start(bf16[2,144,1280]{2,1,0:T(8,128)(2,1)S(1)} %collective-permute-done.peer_y), channel_id=1, source_target_pairs={{0,1},{1,0},{2,3},{3,2},{4,5},{5,4},{6,7},{7,6},{8,9},{9,8},{10,11... | collective-permute-start | bytes 2211848 | tf_op jit(solution)/shard_map/ppermute | solution.py:50
  24.8 12.1 %collective-permute-start.7 = (bf16[144,1280]{1,0:T(8,128)(2,1)S(1)}, bf16[144,1280]{1,0:T(8,128)(2,1)S(1)}, u32[]{:S(2)}, u32[]{:S(2)}) collective-permute-start(bf16[144,1280]{1,0:T(8,128)(2,1)S(1)} %shard_map.141.t0), channel_id=1, source_target_pairs={{0,2},{1,3},{2,0},{3,1},{4,6},{5,7},{6,4},{7,5},{8,10},{9,11},{10,... | collective-permute-start | bytes 1105928 | tf_op jit(solution)/shard_map/ppermute | solution.py:50
  25.2 11.8 %collective-permute-start.6 = (bf16[144,1280]{1,0:T(8,128)(2,1)S(1)}, bf16[144,1280]{1,0:T(8,128)(2,1)S(1)}, u32[]{:S(2)}, u32[]{:S(2)}) collective-permute-start(bf16[144,1280]{1,0:T(8,128)(2,1)S(1)} %shard_map.141.t0), channel_id=1, source_target_pairs={{0,1},{1,0},{2,3},{3,2},{4,5},{5,4},{6,7},{7,6},{8,9},{9,8},{10,11... | collective-permute-start | bytes 1105928 | tf_op jit(solution)/shard_map/ppermute | solution.py:50
  27.4 9.6 %copy-start.3 = (f32[1280]{0:T(1024)S(1)}, f32[1280]{0:T(1024)}, u32[]{:S(2)}) copy-start(f32[1280]{0:T(1024)} %param.20) | copy-start | bytes 15364
  27.4 9.6 %copy-start.4 = (f32[1280]{0:T(1024)S(1)}, f32[1280]{0:T(1024)}, u32[]{:S(2)}) copy-start(f32[1280]{0:T(1024)} %param.21) | copy-start | bytes 15364
  36.9 1.7 %collective-permute-start.10 = (bf16[144,1280]{1,0:T(8,128)(2,1)S(1)}, bf16[144,1280]{1,0:T(8,128)(2,1)S(1)}, u32[]{:S(2)}, u32[]{:S(2)}) collective-permute-start(bf16[144,1280]{1,0:T(8,128)(2,1)S(1)} %collective-permute-done.7.t2), channel_id=1, source_target_pairs={{0,1},{1,0},{2,3},{3,2},{4,5},{5,4},{6,7},{7,6},{8,9},{9,8},{10,11... | collective-permute-start | bytes 1105928 | tf_op jit(solution)/shard_map/ppermute | solution.py:50

commit v4 on v3

--- a/solution.py
+++ b/solution.py
@@ -128,7 +128,7 @@
     zeros = jnp.zeros((4, channels), jnp.float32)
     grouped = join_rows(dot(split_rows(jnp.concatenate([sums, zeros], axis=0)), member)) / count
     mean = grouped[0:2]
-    rstd = lax.rsqrt(grouped[2:4] - mean * mean + 1e-05)
+    rstd = lax.rsqrt(jnp.maximum(grouped[2:4] - mean * mean, 0.0) + 1e-05)
     both = jnp.concatenate([mean, rstd, jnp.zeros((4, 128), jnp.float32)], axis=0)
     return join_rows(
         lax.dot_general(split_rows(both), member, NT, preferred_element_type=jnp.float32)

time: 92.5 us -> 92.5 us (level)
  no operation moved by 1% of the time
where the time goes in v4:
time: 92.5 us; the launch traced here: 92.3 us
  blocking collectives  44.3 us (48%)
  Pallas kernels  22.2 us (24%)
  starting transfers between devices  14.1 us (15%)
  waiting for transfers between devices  9.25 us (10%)
    all_to_all x2, blocking collectives, exchange(): lax.all_to_all(value, 'tm', 0, 0, axis_index_groups=shot_groups(), tiled=...  44.3 us
    pallas_call x6, Pallas kernels, call(): pl.pallas_call(kernel, out_shape=out_shape, grid=(1,), in_specs=in_specs...  22.2 us
    ppermute x11, starting transfers between devices, send(): return lax.ppermute(value, AXES, pairs)  14.1 us
    ppermute x11, waiting for transfers between devices, send(): return lax.ppermute(value, AXES, pairs)  9.25 us
  transfers between devices with their start and end apart: 11, of which 6 were waited for; matrix products, arithmetic and copies ran while one was open for 2% of the time, Pallas kernels for 14%

profile of v4, /device:TPU:2, one launch (start us, length us, event | category | flops | bytes accessed | tf_op | source)
XLA Modules:
  0.0 92.3 jit_solution(11947940037467880508)
XLA Ops:
  0.6 3.3 %collective-permute-start = (bf16[2,144,1280]{2,1,0:T(8,128)(2,1)}, bf16[2,144,1280]{2,1,0:T(8,128)(2,1)S(1)}, u32[]{:S(2)}, u32[]{:S(2)}) collective-permute-start(bf16[2,144,1280]{2,1,0:T(8,128)(2,1)} %bitcast.3), channel_id=1, source_target_pairs={{0,2},{1,3},{2,0},{3,1},{4,6},{5,7},{6,4},{7,5},{8,10},{9,11},{10,... | collective-permute-start | bytes 2211848 | tf_op jit(solution)/shard_map/ppermute | solution.py:50
  3.9 0.0 collective-permute-start.1
  3.9 0.8 constant_dynamic-slice_fusion.codes
  4.7 0.7 collective-permute-done.1
  5.4 0.9 pad_maximum_fusion
  6.2 0.0 copy-start.1
  6.2 0.0 copy-start
  6.2 0.0 copy-start.2
  6.3 2.0 %collective-permute-start.3 = (bf16[36,1280]{1,0:T(8,128)(2,1)S(1)}, bf16[36,1280]{1,0:T(8,128)(2,1)S(1)}, u32[]{:S(2)}, u32[]{:S(2)}) collective-permute-start(bf16[36,1280]{1,0:T(8,128)(2,1)S(1)} %pad_maximum_fusion), channel_id=1, source_target_pairs={{0,4},{1,29},{2,6},{3,31},{4,8},{5,1},{6,10},{7,3},{8,12},{9,5},{1... | collective-permute-start | bytes 276488 | tf_op jit(solution)/shard_map/ppermute | solution.py:50
  8.3 3.3 %collective-permute-start.4 = (bf16[36,1280]{1,0:T(8,128)(2,1)S(1)}, bf16[36,1280]{1,0:T(8,128)(2,1)S(1)}, u32[]{:S(2)}, u32[]{:S(2)}) collective-permute-start(bf16[36,1280]{1,0:T(8,128)(2,1)S(1)} %pad_maximum_fusion), channel_id=1, source_target_pairs={{0,8},{1,25},{2,10},{3,27},{4,12},{5,29},{6,14},{7,31},{8,16},{9,1... | collective-permute-start | bytes 276488 | tf_op jit(solution)/shard_map/ppermute | solution.py:50
  11.5 4.0 %collective-permute-start.5 = (bf16[36,1280]{1,0:T(8,128)(2,1)S(1)}, bf16[36,1280]{1,0:T(8,128)(2,1)S(1)}, u32[]{:S(2)}, u32[]{:S(2)}) collective-permute-start(bf16[36,1280]{1,0:T(8,128)(2,1)S(1)} %pad_maximum_fusion), channel_id=1, source_target_pairs={{0,12},{1,21},{2,14},{3,23},{4,16},{5,25},{6,18},{7,27},{8,20},{9,... | collective-permute-start | bytes 276488 | tf_op jit(solution)/shard_map/ppermute | solution.py:50
  15.6 0.5 collective-permute-start.2
  16.1 4.4 %shard_map.140 = (bf16[1280,1280]{1,0:T(8,128)(2,1)S(1)}, bf16[1280,640]{1,0:T(8,128)(2,1)S(1)}, bf16[640,1280]{1,0:T(8,128)(2,1)S(1)}, bf16[1280,1920]{1,0:T(8,128)(2,1)S(1)}, bf16[16,128]{1,0:T(8,128)(2,1)S(1)}) custom-call(bf16[1280,640]{1,0:T(8,128)(2,1)} %wk.1, bf16[1280,640]{1,0:T(8,128)(2,1)} %wv.1, bf16[1280,640]{1,0:T(8,128)(2,1)} %wq.1, ...), custom_call_target="tpu_custom_call" | custom-call | bytes 11500000 | tf_op jit(solution)/shard_map/pallas_call | solution.py:73
  20.5 3.6 %collective-permute-done.2.far = bf16[18,1280]{1,0:T(8,128)(2,1)S(1)} collective-permute-done((bf16[18,1280]{1,0:T(8,128)(2,1)}, bf16[18,1280]{1,0:T(8,128)(2,1)S(1)}, u32[]{:S(2)}, u32[]{:S(2)}) %collective-permute-start.2) | collective-permute-done | bytes 46112 | tf_op jit(solution)/shard_map/ppermute | solution.py:50
  24.1 0.0 copy-done.1
  24.1 0.0 collective-permute-start.8
  24.1 0.0 collective-permute-done.3.near1
  24.1 0.0 collective-permute-done.4.near2
  24.1 0.0 collective-permute-done.5.near3
  24.1 0.0 copy-done
  24.1 0.1 shard_map.141.t0
  24.2 0.0 collective-permute-done.peer_y
  24.2 0.6 collective-permute-start.9
  24.8 0.0 copy-done.2
  24.8 0.3 collective-permute-start.7
  25.2 0.1 collective-permute-start.6
  25.2 1.1 %collective-permute-done.8.peer_c = bf16[2,144,1280]{2,1,0:T(8,128)(2,1)S(1)} collective-permute-done((bf16[2,144,1280]{2,1,0:T(8,128)(2,1)S(1)}, bf16[2,144,1280]{2,1,0:T(8,128)(2,1)S(1)}, u32[]{:S(2)}, u32[]{:S(2)}) %collective-permute-start.8) | collective-permute-done | bytes 737312 | tf_op jit(solution)/shard_map/ppermute | solution.py:50
  26.3 1.1 %collective-permute-done.9.peer_yc = bf16[2,144,1280]{2,1,0:T(8,128)(2,1)S(1)} collective-permute-done((bf16[2,144,1280]{2,1,0:T(8,128)(2,1)S(1)}, bf16[2,144,1280]{2,1,0:T(8,128)(2,1)S(1)}, u32[]{:S(2)}, u32[]{:S(2)}) %collective-permute-start.9) | collective-permute-done | bytes 737312 | tf_op jit(solution)/shard_map/ppermute | solution.py:50
  27.4 0.0 copy-start.3
  27.4 0.0 copy-start.4
  27.4 8.4 %shard_map.142 = (bf16[288,640]{1,0:T(8,128)(2,1)S(1)}, f32[4,288,256]{2,1,0:T(8,128)S(1)}, f32[288,128]{1,0:T(8,128)S(1)}) custom-call(bf16[2,144,1280]{2,1,0:T(8,128)(2,1)S(1)} %bitcast.5, bf16[2,144,1280]{2,1,0:T(8,128)(2,1)S(1)} %collective-permute-done.8.peer_c, bf16[2,144,1280]{2,1,0:T(8,128)(2,1)S(1)} %collective-permute-done.peer_y, ...), custom_call_target="tpu_custom_call" | custom-call | flops 5400000000 | bytes 9000000 | tf_op jit(solution)/shard_map/pallas_call | solution.py:73
  35.7 1.2 %collective-permute-done.7.t2 = bf16[144,1280]{1,0:T(8,128)(2,1)S(1)} collective-permute-done((bf16[144,1280]{1,0:T(8,128)(2,1)S(1)}, bf16[144,1280]{1,0:T(8,128)(2,1)S(1)}, u32[]{:S(2)}, u32[]{:S(2)}) %collective-permute-start.7) | collective-permute-done | bytes 368672 | tf_op jit(solution)/shard_map/ppermute | solution.py:50
  36.9 0.0 collective-permute-start.10
  36.9 0.0 copy-done.3
  37.0 0.0 copy-done.4
  37.0 0.0 collective-permute-done.6.t1
  37.0 1.6 %collective-permute-done.10.t3 = bf16[144,1280]{1,0:T(8,128)(2,1)S(1)} collective-permute-done((bf16[144,1280]{1,0:T(8,128)(2,1)S(1)}, bf16[144,1280]{1,0:T(8,128)(2,1)S(1)}, u32[]{:S(2)}, u32[]{:S(2)}) %collective-permute-start.10) | collective-permute-done | bytes 368672 | tf_op jit(solution)/shard_map/ppermute | solution.py:50
  38.6 6.1 %shard_map.143 = (bf16[2,144,1280]{2,1,0:T(8,128)(2,1)}, bf16[8,72,640]{2,1,0:T(8,128)(2,1)S(1)}) custom-call(bf16[144,1280]{1,0:T(8,128)(2,1)S(1)} %shard_map.141.t0, bf16[144,1280]{1,0:T(8,128)(2,1)S(1)} %collective-permute-done.6.t1, bf16[144,1280]{1,0:T(8,128)(2,1)S(1)} %collective-permute-done.7.t2, bf16[144,1280]{1,0:T(8,128)(2,1)S(1)} %collective-permute-done.10.t3, ...), custom_call_target="tpu_custom_call" | custom-call | flops 2900000000 | bytes 8000000 | tf_op jit(solution)/shard_map/pallas_call | solution.py:73
  44.7 27.7 %all_to_all.10.moving = bf16[8,72,640]{2,1,0:T(8,128)(2,1)S(1)} all-to-all(bf16[8,72,640]{2,1,0:T(8,128)(2,1)S(1)} %get-tuple-element.38), channel_id=1, replica_groups={{0,4,8,12,16,20,24,28},{32,36,40,44,48,52,56,60},{64,68,72,76,80,84,88,..., dimensions={0} | all-to-all | bytes 1474560 | tf_op jit(solution)/shard_map/all_to_all | solution.py:58
  72.4 2.5 %shard_map.144 = bf16[8,40,640]{2,1,0:T(8,128)(2,1)S(1)} custom-call(bf16[8,72,640]{2,1,0:T(8,128)(2,1)S(1)} %all_to_all.10.moving, bf16[1280,1920]{1,0:T(8,128)(2,1)S(1)} %get-tuple-element.39.weights), custom_call_target="tpu_custom_call" | custom-call | flops 2200000000 | bytes 8000000 | tf_op jit(solution)/shard_map/pallas_call | solution.py:73
  74.9 16.6 %all_to_all.11.packed = bf16[8,40,640]{2,1,0:T(8,128)(2,1)S(1)} all-to-all(bf16[8,40,640]{2,1,0:T(8,128)(2,1)S(1)} %shard_map.144), channel_id=1, replica_groups={{0,4,8,12,16,20,24,28},{32,36,40,44,48,52,56,60},{64,68,72,76,80,84,88,..., dimensions={0} | all-to-all | bytes 819200 | tf_op jit(solution)/shard_map/all_to_all | solution.py:58
  91.5 0.8 shard_map.145
  (3 shorter events, 0.0 us)
Async XLA Ops:
  0.6 23.6 %collective-permute-start = (bf16[2,144,1280]{2,1,0:T(8,128)(2,1)}, bf16[2,144,1280]{2,1,0:T(8,128)(2,1)S(1)}, u32[]{:S(2)}, u32[]{:S(2)}) collective-permute-start(bf16[2,144,1280]{2,1,0:T(8,128)(2,1)} %bitcast.3), channel_id=1, source_target_pairs={{0,2},{1,3},{2,0},{3,1},{4,6},{5,7},{6,4},{7,5},{8,10},{9,11},{10,... | collective-permute-start | bytes 2211848 | tf_op jit(solution)/shard_map/ppermute | solution.py:50
  3.9 1.5 %collective-permute-start.1 = (bf16[18,1280]{1,0:T(8,128)(2,1)}, bf16[18,1280]{1,0:T(8,128)(2,1)S(1)}, u32[]{:S(2)}, u32[]{:S(2)}) collective-permute-start(bf16[18,1280]{1,0:T(8,128)(2,1)} %own.1), channel_id=1, source_target_pairs={{0,1},{1,0},{2,3},{3,2},{4,5},{5,4},{6,7},{7,6},{8,9},{9,8},{10,11... | collective-permute-start | bytes 138248 | tf_op jit(solution)/shard_map/ppermute | solution.py:50
  6.2 17.9 %copy-start.1 = (bf16[2,6,24,1280]{3,2,1,0:T(8,128)(2,1)S(1)}, bf16[2,6,24,1280]{3,2,1,0:T(8,128)(2,1)}, u32[]{:S(2)}) copy-start(bf16[2,6,24,1280]{3,2,1,0:T(8,128)(2,1)} %param.13) | copy-start | bytes 2211844
  6.2 17.9 %copy-start = (bf16[18,1280]{1,0:T(8,128)(2,1)S(1)}, bf16[18,1280]{1,0:T(8,128)(2,1)}, u32[]{:S(2)}) copy-start(bf16[18,1280]{1,0:T(8,128)(2,1)} %own.1) | copy-start | bytes 138244
  6.2 18.6 %copy-start.2 = (f32[1280]{0:T(1024)S(1)}, f32[1280]{0:T(1024)}, u32[]{:S(2)}) copy-start(f32[1280]{0:T(1024)} %param.15) | copy-start | bytes 15364
  6.3 17.8 %collective-permute-start.3 = (bf16[36,1280]{1,0:T(8,128)(2,1)S(1)}, bf16[36,1280]{1,0:T(8,128)(2,1)S(1)}, u32[]{:S(2)}, u32[]{:S(2)}) collective-permute-start(bf16[36,1280]{1,0:T(8,128)(2,1)S(1)} %pad_maximum_fusion), channel_id=1, source_target_pairs={{0,4},{1,29},{2,6},{3,31},{4,8},{5,1},{6,10},{7,3},{8,12},{9,5},{1... | collective-permute-start | bytes 276488 | tf_op jit(solution)/shard_map/ppermute | solution.py:50
  8.3 15.9 %collective-permute-start.4 = (bf16[36,1280]{1,0:T(8,128)(2,1)S(1)}, bf16[36,1280]{1,0:T(8,128)(2,1)S(1)}, u32[]{:S(2)}, u32[]{:S(2)}) collective-permute-start(bf16[36,1280]{1,0:T(8,128)(2,1)S(1)} %pad_maximum_fusion), channel_id=1, source_target_pairs={{0,8},{1,25},{2,10},{3,27},{4,12},{5,29},{6,14},{7,31},{8,16},{9,1... | collective-permute-start | bytes 276488 | tf_op jit(solution)/shard_map/ppermute | solution.py:50
  11.5 12.6 %collective-permute-start.5 = (bf16[36,1280]{1,0:T(8,128)(2,1)S(1)}, bf16[36,1280]{1,0:T(8,128)(2,1)S(1)}, u32[]{:S(2)}, u32[]{:S(2)}) collective-permute-start(bf16[36,1280]{1,0:T(8,128)(2,1)S(1)} %pad_maximum_fusion), channel_id=1, source_target_pairs={{0,12},{1,21},{2,14},{3,23},{4,16},{5,25},{6,18},{7,27},{8,20},{9,... | collective-permute-start | bytes 276488 | tf_op jit(solution)/shard_map/ppermute | solution.py:50
  15.6 8.5 %collective-permute-start.2 = (bf16[18,1280]{1,0:T(8,128)(2,1)}, bf16[18,1280]{1,0:T(8,128)(2,1)S(1)}, u32[]{:S(2)}, u32[]{:S(2)}) collective-permute-start(bf16[18,1280]{1,0:T(8,128)(2,1)} %own.1), channel_id=1, source_target_pairs={{0,16},{1,17},{2,18},{3,19},{4,20},{5,21},{6,22},{7,23},{8,24},{9,... | collective-permute-start | bytes 138248 | tf_op jit(solution)/shard_map/ppermute | solution.py:50
  24.1 2.2 %collective-permute-start.8 = (bf16[2,144,1280]{2,1,0:T(8,128)(2,1)S(1)}, bf16[2,144,1280]{2,1,0:T(8,128)(2,1)S(1)}, u32[]{:S(2)}, u32[]{:S(2)}) collective-permute-start(bf16[2,144,1280]{2,1,0:T(8,128)(2,1)S(1)} %bitcast.4), channel_id=1, source_target_pairs={{0,1},{1,0},{2,3},{3,2},{4,5},{5,4},{6,7},{7,6},{8,9},{9,8},{10,11... | collective-permute-start | bytes 2211848 | tf_op jit(solution)/shard_map/ppermute | solution.py:50
  24.2 3.1 %collective-permute-start.9 = (bf16[2,144,1280]{2,1,0:T(8,128)(2,1)S(1)}, bf16[2,144,1280]{2,1,0:T(8,128)(2,1)S(1)}, u32[]{:S(2)}, u32[]{:S(2)}) collective-permute-start(bf16[2,144,1280]{2,1,0:T(8,128)(2,1)S(1)} %collective-permute-done.peer_y), channel_id=1, source_target_pairs={{0,1},{1,0},{2,3},{3,2},{4,5},{5,4},{6,7},{7,6},{8,9},{9,8},{10,11... | collective-permute-start | bytes 2211848 | tf_op jit(solution)/shard_map/ppermute | solution.py:50
  24.8 12.1 %collective-permute-start.7 = (bf16[144,1280]{1,0:T(8,128)(2,1)S(1)}, bf16[144,1280]{1,0:T(8,128)(2,1)S(1)}, u32[]{:S(2)}, u32[]{:S(2)}) collective-permute-start(bf16[144,1280]{1,0:T(8,128)(2,1)S(1)} %shard_map.141.t0), channel_id=1, source_target_pairs={{0,2},{1,3},{2,0},{3,1},{4,6},{5,7},{6,4},{7,5},{8,10},{9,11},{10,... | collective-permute-start | bytes 1105928 | tf_op jit(solution)/shard_map/ppermute | solution.py:50
  25.2 11.8 %collective-permute-start.6 = (bf16[144,1280]{1,0:T(8,128)(2,1)S(1)}, bf16[144,1280]{1,0:T(8,128)(2,1)S(1)}, u32[]{:S(2)}, u32[]{:S(2)}) collective-permute-start(bf16[144,1280]{1,0:T(8,128)(2,1)S(1)} %shard_map.141.t0), channel_id=1, source_target_pairs={{0,1},{1,0},{2,3},{3,2},{4,5},{5,4},{6,7},{7,6},{8,9},{9,8},{10,11... | collective-permute-start | bytes 1105928 | tf_op jit(solution)/shard_map/ppermute | solution.py:50
  27.4 9.6 %copy-start.3 = (f32[1280]{0:T(1024)S(1)}, f32[1280]{0:T(1024)}, u32[]{:S(2)}) copy-start(f32[1280]{0:T(1024)} %param.20) | copy-start | bytes 15364
  27.4 9.6 %copy-start.4 = (f32[1280]{0:T(1024)S(1)}, f32[1280]{0:T(1024)}, u32[]{:S(2)}) copy-start(f32[1280]{0:T(1024)} %param.21) | copy-start | bytes 15364
  36.9 1.7 %collective-permute-start.10 = (bf16[144,1280]{1,0:T(8,128)(2,1)S(1)}, bf16[144,1280]{1,0:T(8,128)(2,1)S(1)}, u32[]{:S(2)}, u32[]{:S(2)}) collective-permute-start(bf16[144,1280]{1,0:T(8,128)(2,1)S(1)} %collective-permute-done.7.t2), channel_id=1, source_target_pairs={{0,1},{1,0},{2,3},{3,2},{4,5},{5,4},{6,7},{7,6},{8,9},{9,8},{10,11... | collective-permute-start | bytes 1105928 | tf_op jit(solution)/shard_map/ppermute | solution.py:50
